TPU v7x, 128 devices: a whole 4x4x4 slice. The times are simulated.
128 devices in a mesh: lon: 16 (over z_lo, y, core), lat: 4 (over x), ch: 2 (over z_hi).
Axes of the slice: x: 4, y: 4, z: 4 (z_hi: 2, z_lo: 2; z = z_hi * 2 + z_lo), core: 2. Of those that a mesh axis runs over, the one named last changes fastest.
Arguments:
- latents: bfloat16 [4, 64, 64, 2048], P(None, 'ch', 'lat', 'lon'), may hold values from -6 to 6
- conv_weight: bfloat16 [64, 27, 64], P('ch'), may hold values from -0.15625 to 0.15625
- gdn_gamma: float32 [64, 32], P('ch'), may hold values from 0 to 0.1
- gdn_beta: float32 [64], P('ch'), may hold values from 0.5 to 2
- hidden_weight: bfloat16 [128, 640], replicated, may hold values from -0.5 to 0.5
- hidden_bias: float32 [640], replicated, may hold values from -3 to 3
- param_weight: bfloat16 [640, 256], replicated, may hold values from -0.25 to 0.25
- param_bias: float32 [256], replicated, may hold values from -3 to 3
Outputs:
- conv_grad: float32 [64, 1728], P('ch', ('lon', 'lat'))
- hidden_weight_grad: float32 [128, 640], replicated
- hidden_bias_grad: float32 [640], replicated
- param_weight_grad: float32 [640, 256], replicated
- param_bias_grad: float32 [256], replicated
All inputs are finite; a program needn't handle non-finite values.
Results may differ from a plain program's by a relative error of at most 0.0015.
Values may be sent and summed in bfloat16 or wider, within the bound.
A program may use at most 128 MiB of HBM per device.

v0:
```python
import jax
import jax.numpy as jnp
from jax import lax
from jax.sharding import PartitionSpec as P

highest = lax.Precision.HIGHEST


def extended(block, sides, width):
    for axis, dim in sides:
        count = lax.axis_size(axis)
        forward = [(i, i + 1) for i in range(count - 1)]
        forward.append((count - 1, 0))
        backward = [(target, source) for source, target in forward]
        low = lax.ppermute(
            lax.slice_in_dim(block, block.shape[dim] - width, None, axis=dim), axis, forward
        )
        high = lax.ppermute(lax.slice_in_dim(block, 0, width, axis=dim), axis, backward)
        block = jnp.concatenate([low, block, high], axis=dim)
    return block


def entropy_block(
    features, targets, hidden_weight, hidden_bias, param_weight, param_bias, patch_total
):
    pre_act = jnp.dot(features, hidden_weight, preferred_element_type=jnp.float32) + hidden_bias
    hidden = jax.nn.silu(pre_act).astype(jnp.bfloat16)
    params = jnp.dot(hidden, param_weight, preferred_element_type=jnp.float32) + param_bias
    feat_width = features.shape[1]
    centre = params[:, :feat_width]
    raw_spread = params[:, feat_width:]
    spread = 0.5 + jax.nn.softplus(raw_spread)
    scaled_error = (targets.astype(jnp.float32) - centre) / spread
    d_centre = -scaled_error / spread / patch_total
    d_spread = (
        (1.0 - scaled_error * scaled_error) / spread * jax.nn.sigmoid(raw_spread) / patch_total
    )
    d_targets = (scaled_error / spread / patch_total).astype(jnp.bfloat16)
    d_params = jnp.concatenate([d_centre, d_spread], axis=1).astype(jnp.bfloat16)
    grad_pw = jnp.dot(hidden.T, d_params, preferred_element_type=jnp.float32)
    grad_pb = jnp.sum(d_params.astype(jnp.float32), axis=0)
    d_hidden = jnp.dot(d_params, param_weight.T, preferred_element_type=jnp.float32)
    sig_gate = jax.nn.sigmoid(pre_act)
    d_pre = (d_hidden * sig_gate * (1.0 + pre_act * (1.0 - sig_gate))).astype(jnp.bfloat16)
    grad_hw = jnp.dot(features.T, d_pre, preferred_element_type=jnp.float32)
    grad_hb = jnp.sum(d_pre.astype(jnp.float32), axis=0)
    d_features = jnp.dot(d_pre, hidden_weight.T, preferred_element_type=jnp.float32).astype(
        jnp.bfloat16
    )
    return ((grad_hw, grad_hb, grad_pw, grad_pb), d_features, d_targets)


def convolve(source, weight, rows, cols):
    levels = source.shape[0] - 2
    result = jnp.zeros((levels, weight.shape[0], rows, cols), jnp.float32)
    for offset in range(27):
        lev_off, lat_off, lon_off = (offset // 9, offset // 3 % 3, offset % 3)
        window = source[
            lev_off : lev_off + levels, :, lat_off : lat_off + rows, lon_off : lon_off + cols
        ]
        result = result + jnp.einsum(
            "oc,lcab->loab", weight[:, offset, :], window, preferred_element_type=jnp.float32
        )
    return result


def weight_terms(d_conv, source, rows, cols):
    levels = source.shape[0] - 2
    tap_grads = []
    for offset in range(27):
        lev_off, lat_off, lon_off = (offset // 9, offset // 3 % 3, offset % 3)
        window = source[
            lev_off : lev_off + levels, :, lat_off : lat_off + rows, lon_off : lon_off + cols
        ]
        tap_grads.append(
            jnp.einsum("loab,lcab->oc", d_conv, window, preferred_element_type=jnp.float32)
        )
    return jnp.stack(tap_grads, axis=1).reshape(d_conv.shape[1], -1)


def on_device(
    latents, conv_weight, gdn_gamma, gdn_beta, hidden_weight, hidden_bias, param_weight, param_bias
):
    levels, group_width, band_rows, cycle_cols = latents.shape
    feat_width = 4 * group_width
    padded = extended(latents, (("lon", 3), ("lat", 2)), 1)
    row_index = lax.broadcasted_iota(jnp.int32, (1, 1, band_rows + 2, 1), 2)
    band_index = lax.axis_index("lat")
    last_band = lax.axis_size("lat") - 1
    outside = (row_index == 0) & (band_index == 0) | (row_index == band_rows + 1) & (
        band_index == last_band
    )
    padded = jnp.where(outside, jnp.zeros_like(padded), padded)
    gathered = lax.all_gather(padded, "ch", axis=1, tiled=True)
    gathered = jnp.pad(gathered, ((1, 1), (0, 0), (0, 0), (0, 0)))
    conv_out = convolve(gathered, conv_weight, band_rows, cycle_cols)
    denominator = gdn_beta[None, :, None, None] + jnp.einsum(
        "oj,ljab->loab", gdn_gamma, conv_out * conv_out, precision=highest
    )
    inv_root = lax.rsqrt(denominator)
    normed = (conv_out * inv_root).astype(jnp.bfloat16)
    patches = normed.reshape(levels, group_width, band_rows // 2, 2, cycle_cols // 2, 2)
    patches = jnp.transpose(patches, (0, 2, 4, 3, 5, 1)).reshape(-1, feat_width)
    patch_count = patches.shape[0]
    patch_total = patch_count * lax.axis_size("lon") * lax.axis_size("lat")
    senders = lax.axis_size("lon") * lax.axis_size("ch")
    pieces = patches.reshape(senders, patch_count // senders, feat_width)
    arrived = lax.all_to_all(pieces, ("lon", "ch"), split_axis=0, concat_axis=0, tiled=True)
    arrived = arrived.reshape(senders // 2, 2, patch_count // senders, feat_width)
    features = arrived[:, 0].reshape(-1, feat_width)
    targets = arrived[:, 1].reshape(-1, feat_width)
    grads, d_features, d_targets = entropy_block(
        features, targets, hidden_weight, hidden_bias, param_weight, param_bias, patch_total
    )
    returned = jnp.stack(
        [
            d_features.reshape(senders // 2, patch_count // senders, feat_width),
            d_targets.reshape(senders // 2, patch_count // senders, feat_width),
        ],
        axis=1,
    )
    returned = returned.reshape(senders, patch_count // senders, feat_width)
    came_back = lax.all_to_all(returned, ("lon", "ch"), split_axis=0, concat_axis=0, tiled=True)
    d_patches = came_back.reshape(levels, band_rows // 2, cycle_cols // 2, 2, 2, group_width)
    d_normed = (
        jnp.transpose(d_patches, (0, 5, 1, 3, 2, 4))
        .reshape(levels, group_width, band_rows, cycle_cols)
        .astype(jnp.float32)
    )
    weighted = d_normed * conv_out * inv_root / denominator
    d_conv = (
        d_normed * inv_root
        - conv_out * jnp.einsum("co,lcab->loab", gdn_gamma, weighted, precision=highest)
    ).astype(jnp.bfloat16)
    local_grad = weight_terms(d_conv, gathered, band_rows, cycle_cols)
    summed = lax.psum((grads[0], grads[1], grads[2], grads[3]), ("lon", "lat", "ch"))
    conv_grad = lax.psum_scatter(local_grad, ("lon", "lat"), scatter_dimension=1, tiled=True)
    return (conv_grad, summed[0], summed[1], summed[2], summed[3])


def solution(mesh):
    placed = (
        P(None, "ch", "lat", "lon"),
        P("ch", None, None),
        P("ch", None),
        P("ch"),
        P(),
        P(),
        P(),
        P(),
    )
    return jax.shard_map(
        on_device,
        mesh=mesh,
        in_specs=placed,
        out_specs=(P("ch", ("lon", "lat")), P(), P(), P(), P()),
        check_vma=False,
    )
```

profile of v0, /device:TPU:1, one launch (start us, length us, event | category | flops | bytes accessed | tf_op | source)
XLA Modules:
  0.0 818.2 jit_solution(1389502294937117656)
XLA Ops:
  7.2 1.2 copy.139
  8.7 2.8 collective-permute-start
  11.4 6.1 collective-permute-done
  17.6 2.8 collective-permute-done.1
  20.5 1.3 collective-permute-start.2
  21.8 1.5 collective-permute-start.3
  23.2 1.6 collective-permute-done.2
  24.9 1.7 maximum_select_fusion
  26.6 43.4 %all-gather.2.cloned.1.call-done = bf16[4,64,18,130]{3,1,2,0:T(8,128)(2,1)} async-done(((bf16[4,32,18,130]{3,1,2,0:T(8,128)(2,1)}), bf16[4,64,18,130]{3,1,2,0:T(8,128)(2,1)}) %all-gather.2.cloned.1.call-update) | async-done | bytes 1198096 | tf_op jit(solution)/shard_map/all_gather | solution.py:94
  70.0 1.6 fusion.106
  84.6 2.3 fusion.73
  86.9 1.7 copy.142
  88.6 5.8 copy.143
  94.4 2.3 copy.144
  96.8 5.6 all-to-all-start
  102.4 9.4 %pad_slice_fusion = (bf16[4,64,16,128]{3,1,2,0:T(8,128)(2,1)}, bf16[4,64,16,128]{3,1,2,0:T(8,128)(2,1)}, bf16[4,64,16,128]{3,1,2,0:T(8,128)(2,1)}, bf16[4,64,16,...) fusion(bf16[4,64,18,130]{3,1,2,0:T(8,128)(2,1)S(1)} %copy-done.1), kind=kLoop, calls=%fused_computation | loop fusion | bytes 24379392 | tf_op jit(solution)/shard_map/slice | solution.py:58
  111.8 2.0 all-to-all-done
  116.2 1.3 convert_reduce_fusion
  119.9 5.4 all-to-all-start.1
  125.6 4.1 fusion.173
  129.7 1.4 fusion.77
  131.1 5.6 all-to-all-done.1
  137.1 4.4 copy.148
  141.5 2.9 copy.149
  144.5 1.3 fusion.14
  159.7 1.1 fusion.176
  162.3 65.1 %all-reduce.2 = (f32[640]{0:T(1024)}, f32[256]{0:T(256)}) all-reduce(f32[640]{0:T(1024)S(1)} %get-tuple-element.49, f32[256]{0:T(256)S(1)} %convert_reduce_fusion.1), channel_id=1, replica_groups=mesh['lon'=16,'lat'=4,'ch'=2] {'lon','lat','ch'}, use_global_device_ids=true, to_apply=%region_3.4 | all-reduce | flops 896 | bytes 7168 | tf_op jit(solution)/shard_map/psum | solution.py:136
  227.4 427.0 %all-reduce.7.cloned.1.call-done = f32[32,1728]{1,0:T(8,128)} async-done(((f32[32,1728]{1,0:T(8,128)}), f32[32,1728]{1,0:T(8,128)}) %all-reduce.7.cloned.1.call-update) | async-done | bytes 221200
  654.4 1.4 constant_dynamic-slice_fusion
  655.8 152.2 %all-reduce.9.cloned.1.call-done = (f32[128,640]{1,0:T(8,128)}, f32[640,256]{1,0:T(8,128)}) async-done(((f32[128,640]{1,0:T(8,128)}, f32[640,256]{1,0:T(8,128)}), (f32[128,640]{1,0:T(8,128)}, f32[640,256]{1,0:T(8,128)})) %all-reduce.9.cloned.1.call-update) | async-done | bytes 983056 | tf_op jit(solution)/shard_map/psum | solution.py:136
  808.0 1.7 copy.403
  809.7 2.0 copy.404
  (177 shorter events, 33.2 us)
Async XLA Ops:
  7.2 107.6 %copy-start = (bf16[640,256]{1,0:T(8,128)(2,1)S(1)}, bf16[640,256]{1,0:T(8,128)(2,1)}, u32[]{:S(2)}) copy-start(bf16[640,256]{1,0:T(8,128)(2,1)} %param.14) | copy-start | bytes 983044
  7.2 62.8 %all-gather.2.cloned.1.call-start = ((), (), s32[]{:S(2)}) async-start(), calls=%async_computation.2 | async-start | bytes 3538944 | tf_op jit(solution)/shard_map/all_gather | solution.py:94
  8.7 8.9 %collective-permute-start = (bf16[4,32,16,1]{3,1,2,0:T(8,128)(2,1)S(1)}, bf16[4,32,16,1]{3,1,2,0:T(8,128)(2,1)S(1)}, u32[]{:S(2)}, u32[]{:S(2)}) collective-permute-start(bf16[4,32,16,1]{3,1,2,0:T(8,128)(2,1)S(1)} %get-tuple-element.43), channel_id=1, source_target_pairs={{0,8},{8,16},{16,24},{24,32},{32,40},{40,48},{48,56},{56,64},{64,7... | collective-permute-start | bytes 12296 | tf_op jit(solution)/shard_map/ppermute | solution.py:15
  11.4 8.9 %collective-permute-start.1 = (bf16[4,32,16,1]{3,1,2,0:T(8,128)(2,1)S(1)}, bf16[4,32,16,1]{3,1,2,0:T(8,128)(2,1)S(1)}, u32[]{:S(2)}, u32[]{:S(2)}) collective-permute-start(bf16[4,32,16,1]{3,1,2,0:T(8,128)(2,1)S(1)} %get-tuple-element.44), channel_id=1, source_target_pairs={{8,0},{16,8},{24,16},{32,24},{40,32},{48,40},{56,48},{64,56},{72,6... | collective-permute-start | bytes 12296 | tf_op jit(solution)/shard_map/ppermute | solution.py:18
  20.5 49.5 %copy-start.43 = (bf16[32,27,64]{2,0,1:T(8,128)(2,1)S(1)}, bf16[32,27,64]{2,0,1:T(8,128)(2,1)}, u32[]{:S(2)}) copy-start(bf16[32,27,64]{2,0,1:T(8,128)(2,1)} %param.9) | copy-start | bytes 331780
  20.5 4.4 collective-permute-start.2
  21.8 3.1 collective-permute-start.3
  70.0 1.9 copy-start.1
  83.0 1.6 copy-start.46
  83.1 1.6 copy-start.48
  96.8 17.1 %all-to-all-start = ((bf16[32,64,128]{2,1,0:T(8,128)(2,1)}), bf16[32,64,128]{2,1,0:T(8,128)(2,1)S(1)}, u32[]{:S(2)}, u32[]{:S(2)}) async-start(bf16[32,64,128]{2,1,0:T(8,128)(2,1)} %copy.144), calls=%async_computation | async-start | bytes 1048576 | tf_op jit(solution)/shard_map/all_to_all | solution.py:108
  102.4 11.5 %copy-start.44 = (bf16[128,640]{1,0:T(8,128)(2,1)S(1)}, bf16[128,640]{1,0:T(8,128)(2,1)}, u32[]{:S(2)}) copy-start(bf16[128,640]{1,0:T(8,128)(2,1)} %param.12) | copy-start | bytes 491524
  102.4 11.5 %copy-start.49 = (f32[640]{0:T(1024)S(1)}, f32[640]{0:T(1024)}, u32[]{:S(2)}) copy-start(f32[640]{0:T(1024)} %param.13) | copy-start | bytes 7684
  116.1 13.6 %copy-start.36 = (bf16[1024,128]{1,0:T(8,128)(2,1)}, bf16[1024,128]{1,0:T(8,128)(2,1)S(1)}, u32[]{:S(2)}) copy-start(bf16[1024,128]{1,0:T(8,128)(2,1)S(1)} %get-tuple-element.38) | copy-start | bytes 786436
  116.1 2.4 copy-start.45
  119.9 16.8 %all-to-all-start.1 = ((bf16[32,64,128]{2,1,0:T(8,128)(2,1)}), bf16[32,64,128]{2,1,0:T(8,128)(2,1)S(1)}, u32[]{:S(2)}, u32[]{:S(2)}) async-start(bf16[32,64,128]{2,1,0:T(8,128)(2,1)} %bitcast.507), calls=%async_computation.1 | async-start | bytes 1048576 | tf_op jit(solution)/shard_map/all_to_all | solution.py:123
  125.3 529.1 %all-reduce.7.cloned.1.call-start = ((), (), s32[]{:S(2)}) async-start(), calls=%async_computation.3 | async-start | bytes 458752
  125.6 4.1 copy-start.7
  125.6 4.1 copy-start.39
  141.5 3.0 copy-start.5
  141.5 3.0 copy-start.35
  144.5 1.7 copy-start.26
  145.8 1.7 copy-start.24
  146.2 1.7 copy-start.23
  147.8 1.4 copy-start.20
  148.8 1.4 copy-start.33
  157.9 1.8 copy-start.3
  157.9 1.8 copy-start.42
  158.5 2.4 copy-start.50
  158.5 3.7 copy-start.37
  158.5 3.6 copy-start.40
  159.7 648.3 %all-reduce.9.cloned.1.call-start = ((), (), s32[]{:S(2)}) async-start(), calls=%async_computation.4 | async-start | bytes 1966080 | tf_op jit(solution)/shard_map/psum | solution.py:136
  (28 other events, 36.8 us)
Sparse Core Ops, SparseCore 0:
  26.7 43.2 all-gather.1
  159.8 494.5 all-reduce.6
  660.5 147.4 all-reduce.8
where the time goes:
time: 819 us; the launch traced here: 818 us
  waiting for transfers between devices  641 us (78%)
  blocking collectives  65.1 us (8%)
  local copies, waits for them, and re-layouts  43.8 us (5%)
  matrix products  33.1 us (4%)
  starting transfers between devices  16.8 us (2%)
  between operations  15.1 us (2%)
    unnamed x4, waiting for transfers between devices  427 us
    psum x1, waiting for transfers between devices, on_device(): lax.psum((grads[0], grads[1], grads[2], grads[3]), ('lon', 'lat', 'ch'))  152 us
    psum x1, blocking collectives, on_device(): lax.psum((grads[0], grads[1], grads[2], grads[3]), ('lon', 'lat', 'ch'))  65.1 us
    all_gather x1, waiting for transfers between devices, on_device(): gathered = lax.all_gather(padded, 'ch', axis=1, tiled=True)  43.4 us
  transfers between devices with their start and end apart: 9, of which 8 were waited for; matrix products, arithmetic and copies ran while one was open for 2% of the time, Pallas kernels for 0%

commit v1 on v0

v1 whole, which is shorter than its diff:
```python
import jax
import jax.numpy as jnp
from jax import lax
from jax.experimental import pallas as pl
from jax.experimental.pallas import tpu as pltpu
from jax.sharding import PartitionSpec as P

BF = jnp.bfloat16
F32 = jnp.float32
MESH = pl.DeviceIdType.MESH
PATCHES = 131072.0

NN = (((1,), (0,)), ((), ()))
NT = (((1,), (1,)), ((), ()))


def mm(a, b, dims=NN):
    return lax.dot_general(a, b, dims, preferred_element_type=F32)


def iota(shape, dim):
    return lax.broadcasted_iota(jnp.int32, shape, dim)


def onehot(condition):
    return jnp.where(condition, 1.0, 0.0).astype(BF)


def split(value):
    high = value.astype(BF)
    return high, (value - high.astype(F32)).astype(BF)


class Place:
    def __init__(self):
        self.lon = lax.axis_index("lon")
        self.lat = lax.axis_index("lat")
        self.ch = lax.axis_index("ch")
        self.core = self.lon % 2
        self.y = (self.lon // 2) % 4
        self.zlo = self.lon // 8
        self.x = self.lat
        self.z = self.ch * 2 + self.zlo

    def chip(self, x, y, z, core):
        return ((z % 2) * 8 + y * 2 + core, x, z // 2)

    def sibling(self):
        return self.chip(self.x, self.y, self.z, 1 - self.core)

    def along_x(self, d):
        return self.chip((self.x + d) % 4, self.y, self.z, self.core)

    def along_y(self, d):
        return self.chip(self.x, (self.y + d) % 4, self.z, self.core)

    def along_z(self, d):
        return self.chip(self.x, self.y, (self.z + d) % 4, self.core)

    def along_first(self, d):
        on_x = 1 - self.core
        return self.chip(
            (self.x + d * on_x) % 4, (self.y + d * (1 - on_x)) % 4, self.z, self.core
        )

    def along_second(self, d):
        on_x = self.core
        return self.chip(
            (self.x + d * on_x) % 4, (self.y + d * (1 - on_x)) % 4, self.z, self.core
        )


def remote(src, dst, send, recv, device):
    return pltpu.make_async_remote_copy(
        src_ref=src,
        dst_ref=dst,
        send_sem=send,
        recv_sem=recv,
        device_id=device,
        device_id_type=MESH,
    )


def enter(place):
    lon, lat, ch = place.lon, place.lat, place.ch
    barrier = pltpu.get_barrier_semaphore()
    row = lat + 2 * ch - 1
    row = (row + 4) % 4
    sources = [(lon, lat, 1 - ch), (lon, row, 0), (lon, row, 1)]
    for side in (1, 15):
        for other in (0, 1):
            sources.append(((lon + side) % 16, lat, other))
            sources.append(((lon + side) % 16, row, other))
    sources.append(place.sibling())
    for d in (1, 2, 3):
        sources += [place.along_x(d), place.along_y(d), place.along_z(d)]
    for device in sources:
        pl.semaphore_signal(barrier, inc=1, device_id=device, device_id_type=MESH)
    return barrier, len(sources)


def shuffle_latents(x_ref, own, rim_out):
    rows, cols = iota((512, 512), 0), iota((512, 512), 1)
    swap = onehot(cols == (rows % 32) * 16 + rows // 32)
    b, n = iota((128, 256), 0), iota((128, 256), 1)
    parity = jnp.where(n < 64, 2 * n, 2 * (n - 64) + 1)
    edge = jnp.where(n < 192, 0, 127)
    spread = onehot(b == jnp.where(n < 128, parity, edge))
    r, j = iota((512, 128), 0), iota((512, 128), 1)
    rims = jnp.zeros((512, 128), F32)
    sorted_levels = []
    for level in range(4):
        block = mm(x_ref[level].reshape(512, 128), spread)
        rims = jnp.where((j % 64) == (r % 16) * 4 + level, block[:, 128:], rims)
        sorted_levels.append(block[:, :128].astype(BF))
    for level in range(4):
        own[:, level] = mm(swap, sorted_levels[level]).astype(BF).reshape(16, 32, 128)
    c, k = iota((32, 512), 0), iota((32, 512), 1)
    rim_out[...] = mm(onehot(k // 16 == c), rims.astype(BF)).astype(BF)


def prepare_small(hw_ref, hb_ref, pw_ref, pb_ref, hwt, pwt, hbt, pbt):
    eye = onehot(iota((128, 128), 0) == iota((128, 128), 1))
    for k in range(5):
        part = slice(128 * k, 128 * k + 128)
        hwt[part, :] = mm(eye, hw_ref[:, part], NT).astype(BF)
        hbt[part, :] = jnp.broadcast_to(hb_ref[:, part], (128, 128)).T
    for k in range(2):
        part = slice(128 * k, 128 * k + 128)
        pwt[part, :] = mm(eye, pw_ref[:, part], NT).astype(BF)
        pbt[part, :] = jnp.broadcast_to(pb_ref[:, part], (128, 128)).T


def build_gamma(gall, gam, gamt, beta):
    k, n = iota((128, 256), 0), iota((128, 256), 1)
    copies = onehot(k == n % 32)
    for g in range(2):
        high, low = split(gall[g])
        for which, part in ((0, high), (1, low)):
            wide = mm(part, copies)
            for s in range(4):
                block = g * 4 + s
                own_block = iota((32, 256), 1) // 32 == block
                gam[which, block * 32 : block * 32 + 32, :] = jnp.where(own_block, wide, 0.0)
        for s in range(4):
            block = g * 4 + s
            beta[block * 32 : block * 32 + 32, :] = jnp.broadcast_to(
                gall[g][:, 64:65], (32, 256)
            )
    for which in range(2):
        gamt[which] = gam[which].T


def build_weights(wall, wf):
    lane = iota((32, 256), 1)
    for g in range(2):
        for n in range(9):
            dl, da = n // 3, n % 3
            base = (192 * n) // 128 * 128
            v = wall[g, :, base : base + 256].astype(F32)
            first = v if n % 2 == 0 else pltpu.roll(v, 192, 1)
            second = v if n % 2 == 1 else pltpu.roll(v, 64, 1)
            first = jnp.where(lane < 192, first, 0.0).astype(BF)
            second = jnp.where(lane >= 64, second, 0.0).astype(BF)
            for p in range(2):
                r = da + p
                row = g * 128 + 2 * p * 32
                wf[dl, row : row + 32, 256 * r : 256 * r + 256] = first
                wf[dl, row + 32 : row + 64, 256 * r : 256 * r + 256] = second
        for dl in range(3):
            for p in range(2):
                r = 3 if p == 0 else 0
                row = g * 128 + 2 * p * 32
                wf[dl, row : row + 64, 256 * r : 256 * r + 256] = jnp.zeros((64, 256), BF)


def build_windows(place, field, rim_in, rims, xt):
    chi, lat = place.ch, place.lat
    k, n = iota((512, 128), 0), iota((512, 128), 1)
    block, kk, nn = k // 128, k % 128, n % 64
    left = block < 2
    same = block % 2 == 0
    pole = jnp.where(chi == 0, lat, 3 - lat) == 0
    shift_same = (8 * chi - 1) * 4
    other_low = 36 * chi
    shift_other = jnp.where(chi == 0, 60, -36)
    shift = jnp.where(same, shift_same, shift_other)
    source = nn + shift
    inside = (source >= 0) & (source < 64) & (nn < 40)
    only = (nn >= other_low) & (nn < other_low + 4) & jnp.logical_not(pole)
    valid = inside & (same | only)
    side = (left & (n < 64)) | (jnp.logical_not(left) & (n >= 64))
    chosen = kk == source + jnp.where(left, 64, 0)
    pick = onehot(valid & side & chosen)
    tiles = jnp.concatenate(
        [rim_in[s, t].reshape(64, 128) for s in range(2) for t in range(2)], axis=1
    )
    rims[...] = mm(tiles, pick)

    col = iota((1, 512), 1)
    w, js, m = col // 128, (col % 128) // 64, col % 64
    target = jnp.where(
        w == 0,
        jnp.where(m == 0, 256 + js * 8, js * 128 + 63 + m),
        jnp.where(
            w == 1,
            js * 128 + m,
            jnp.where(
                w == 2,
                js * 128 + 64 + m,
                jnp.where(m == 63, 320 + js * 8, js * 128 + m + 1),
            ),
        ),
    )
    pick2 = onehot(iota((384, 512), 0) == target)
    for r in range(4):
        for pair in range(2):
            j0 = r + 4 * pair
            j1 = j0 + 2
            stack = []
            for level in range(4):
                edge = pltpu.roll(rims[...], 128 - (j0 * 4 + level), 1).astype(BF)
                stack.append(
                    jnp.concatenate(
                        [
                            field[j0, level].reshape(64, 128),
                            field[j1, level].reshape(64, 128),
                            edge,
                        ],
                        axis=1,
                    )
                )
            out = mm(jnp.concatenate(stack, axis=0), pick2).astype(BF)
            for level in range(4):
                for v in range(4):
                    lane = level * 256 + pair * 128
                    xt[r * 256 + v * 64 : r * 256 + v * 64 + 64, lane : lane + 128] = out[
                        level * 64 : level * 64 + 64, v * 128 : v * 128 + 128
                    ]


def mix(gam, value):
    high, low = split(value)
    ghigh, glow = gam[0].astype(BF), gam[1].astype(BF)
    return mm(ghigh, high) + (mm(ghigh, low) + mm(glow, high))


def forward(s):
    for level in range(4):
        lanes = slice(256 * level, 256 * level + 256)
        total = None
        for dl in range(3):
            other = level + dl - 1
            if 0 <= other < 4:
                term = mm(s["wf"][dl], s["xt"][:, 256 * other : 256 * other + 256])
                total = term if total is None else total + term
        s["conv"][:, lanes] = total
    for level in range(4):
        lanes = slice(256 * level, 256 * level + 256)
        total = s["conv"][:, lanes]
        inv = lax.rsqrt(s["beta"][...] + mix(s["gam"], total * total))
        s["inv"][:, lanes] = inv
        s["normed"][:, lanes] = (total * inv).astype(BF)


def entropy(s, hw_ref, pw_ref):
    def first(i, carry):
        lanes = pl.ds(pl.multiple_of(i * 256, 256), 256)
        features = s["normed"][0:128, lanes]
        for k in range(5):
            part = slice(128 * k, 128 * k + 128)
            bias = s["hbt"][part, :]
            pre = mm(s["hwt"][part, :], features) + jnp.concatenate([bias, bias], axis=1)
            sig = 1.0 / (1.0 + jnp.exp(-pre))
            act = pre * sig
            s["hidden"][part, lanes] = act.astype(BF)
            s["gate"][part, lanes] = sig * (1.0 + pre - act)
        return carry

    lax.fori_loop(0, 4, first, 0)

    def second(i, carry):
        lanes = pl.ds(pl.multiple_of(i * 256, 256), 256)
        hidden = s["hidden"][:, lanes]
        cb, rb = s["pbt"][0:128, :], s["pbt"][128:256, :]
        centre = mm(s["pwt"][0:128, :], hidden) + jnp.concatenate([cb, cb], axis=1)
        raw = mm(s["pwt"][128:256, :], hidden) + jnp.concatenate([rb, rb], axis=1)
        small = jnp.exp(-jnp.abs(raw))
        spread = 0.5 + jnp.maximum(raw, 0.0) + jnp.log1p(small)
        sig = jnp.where(raw >= 0.0, 1.0, small) / (1.0 + small)
        over = 1.0 / spread
        error = (s["normed"][128:256, lanes].astype(F32) - centre) * over
        ratio = error * over * (1.0 / PATCHES)
        s["dparams"][0:128, lanes] = (-ratio).astype(BF)
        s["dparams"][128:256, lanes] = (
            (1.0 - error * error) * over * sig * (1.0 / PATCHES)
        ).astype(BF)
        s["dtargets"][:, lanes] = ratio.astype(BF)
        return carry

    lax.fori_loop(0, 4, second, 0)

    ones = jnp.ones((8, 1024), BF)
    grad = mm(s["hidden"][...], s["dparams"][...], NT)
    part = s["part"]
    for half in range(2):
        block = grad[:, 128 * half : 128 * half + 128]
        part[40 * half : 40 * half + 40] = block.reshape(40, 16, 128)
    pb = mm(ones, s["dparams"][...], NT)

    def third(i, carry):
        lanes = pl.ds(pl.multiple_of(i * 256, 256), 256)
        back = mm(pw_ref[...], s["dparams"][:, lanes])
        s["dpre"][:, lanes] = (back * s["gate"][:, lanes]).astype(BF)
        return carry

    lax.fori_loop(0, 4, third, 0)
    grad = mm(s["normed"][0:128, :], s["dpre"][...], NT)
    for k in range(5):
        block = grad[:, 128 * k : 128 * k + 128]
        part[80 + 8 * k : 88 + 8 * k] = block.reshape(8, 16, 128)
    hb = mm(ones, s["dpre"][...], NT)
    zeros = jnp.zeros((1, 128), F32)
    lines = [hb[0:1, 128 * k : 128 * k + 128] for k in range(5)]
    lines += [pb[0:1, 0:128], pb[0:1, 128:256]] + [zeros] * 9
    part[120] = jnp.concatenate(lines, axis=0)
    part[121:128] = jnp.zeros((7, 16, 128), F32)


def backward(s, hw_ref):
    for level in range(4):
        lanes = slice(256 * level, 256 * level + 256)
        dfeat = mm(hw_ref[...], s["dpre"][:, lanes]).astype(BF).astype(F32)
        dn = jnp.concatenate([dfeat, s["dtargets"][:, lanes].astype(F32)], axis=0)
        inv = s["inv"][:, lanes]
        y = s["conv"][:, lanes]
        dni = dn * inv
        weighted = dni * y * (inv * inv)
        s["dconv"][:, lanes] = (dni - y * mix(s["gamt"], weighted)).astype(BF)
    for dl in range(3):
        first, last = max(0, 1 - dl), min(4, 5 - dl)
        d = s["dconv"][:, 256 * first : 256 * last]
        x = s["xt"][:, 256 * (first + dl - 1) : 256 * (last + dl - 1)]
        s["taps"][dl] = mm(d, x, NT)
    for dl in range(3):
        for da in range(3):
            n = dl * 3 + da
            for g in range(2):
                total = None
                for p in range(2):
                    row = g * 128 + 2 * p * 32
                    lanes = slice(256 * (da + p), 256 * (da + p) + 256)
                    a = s["taps"][dl, row : row + 32, lanes]
                    b = s["taps"][dl, row + 32 : row + 64, lanes]
                    term = a + pltpu.roll(b, 192, 1)
                    total = term if total is None else total + term
                s["wgrad"][32 * g : 32 * g + 32, 192 * n : 192 * n + 192] = total[:, 0:192]
    s["wgrad"][:, 1728:2048] = jnp.zeros((64, 320), F32)
    for k in range(16):
        start = 108 * k
        base = start // 128 * 128
        shift = (256 - (start - base)) % 256
        v = s["wgrad"][:, base : base + 256]
        v = pltpu.roll(v, shift, 1)[:, 0:128] if shift else v[:, 0:128]
        core, y, zlo = k % 2, (k // 2) % 4, k // 8
        for g in range(2):
            s["cpart"][core, g * 2 + zlo, y] = v[32 * g : 32 * g + 32, :]


def body(
    x_ref, wl_ref, gb_ref, hw_ref, hb_ref, pw_ref, pb_ref,
    cg_ref, hwg_ref, hbg_ref, pwg_ref, pbg_ref,
    own, rim_out, rim_in, field, wall, gall, rims,
    xt, wf, gam, gamt, beta, hwt, pwt, hbt, pbt,
    conv, inv, normed, hidden, gate, dparams, dtargets, dpre, dconv, taps, wgrad,
    part, cpart, total, r1, r2, r3, r4, q1, q2, q3, q4,
    local_sem, xs, xr, as_, ar, cs, cr,
):
    place = Place()
    lon, lat, chi = place.lon, place.lat, place.ch
    partner = (lon, lat, 1 - chi)
    barrier, count = enter(place)

    locals_ = [
        pltpu.make_async_copy(wl_ref, wall.at[chi], local_sem.at[0]),
        pltpu.make_async_copy(gb_ref, gall.at[chi], local_sem.at[1]),
    ]
    for copy in locals_:
        copy.start()
    shuffle_latents(x_ref, own, rim_out)
    pl.semaphore_wait(barrier, count)

    sends = []
    sends.append(
        remote(
            own.at[pl.ds(7 * (1 - chi), 9)],
            field.at[pl.ds(chi, 9), :, chi],
            xs.at[0], xr.at[0], partner,
        )
    )
    sends.append(remote(wl_ref, wall.at[chi], xs.at[1], xr.at[1], partner))
    sends.append(remote(gb_ref, gall.at[chi], xs.at[2], xr.at[2], partner))
    down, up = (lat + 3) % 4, (lat + 1) % 4
    sends.append(
        remote(own.at[0], field.at[9, :, chi], xs.at[3], xr.at[3 + chi], (lon, down, 1))
    )
    sends.append(
        remote(own.at[15], field.at[0, :, chi], xs.at[4], xr.at[3 + chi], (lon, up, 0))
    )
    for side in range(2):
        near = (lon + 1) % 16 if side == 0 else (lon + 15) % 16
        for kind, (row, half) in enumerate(((lat, 0), (lat, 1), (down, 1), (up, 0))):
            other = kind // 2
            slot = 5 + (side * 2 + other) * 2
            sends.append(
                remote(
                    rim_out,
                    rim_in.at[side, other, chi],
                    xs.at[5 + side * 4 + kind], xr.at[slot + chi], (near, row, half),
                )
            )
    for copy in sends:
        copy.start()
    mine = pltpu.make_async_copy(
        own.at[pl.ds(7 * chi, 9)], field.at[pl.ds(1 - chi, 9), :, chi], local_sem.at[2]
    )
    mine.start()
    prepare_small(hw_ref, hb_ref, pw_ref, pb_ref, hwt, pwt, hbt, pbt)
    for copy in locals_:
        copy.wait()
    mine.wait()
    other = 1 - chi
    remote(gb_ref, gall.at[other], xs.at[2], xr.at[2], partner).wait_recv()
    build_gamma(gall, gam, gamt, beta)
    remote(wl_ref, wall.at[other], xs.at[1], xr.at[1], partner).wait_recv()
    build_weights(wall, wf)
    for half in range(2):
        remote(
            own.at[0], field.at[9 * chi, :, half], xs.at[3], xr.at[3 + half], partner
        ).wait_recv()
    for side in range(2):
        for kind in range(2):
            for half in range(2):
                remote(
                    rim_out, rim_in.at[side, kind, half], xs.at[5],
                    xr.at[5 + (side * 2 + kind) * 2 + half], partner,
                ).wait_recv()
    remote(
        own.at[pl.ds(0, 9)], field.at[pl.ds(1 - chi, 9), :, other], xs.at[0], xr.at[0], partner
    ).wait_recv()

    @pl.when(jnp.where(chi == 0, lat, 3 - lat) == 0)
    def _():
        field[9 * chi] = jnp.zeros(field.shape[1:], BF)

    build_windows(place, field, rim_in, rims, xt)
    s = {
        "xt": xt, "wf": wf, "gam": gam, "gamt": gamt, "beta": beta, "hwt": hwt, "pwt": pwt,
        "hbt": hbt, "pbt": pbt, "conv": conv, "inv": inv, "normed": normed, "hidden": hidden,
        "gate": gate, "dparams": dparams, "dtargets": dtargets, "dpre": dpre, "dconv": dconv,
        "taps": taps, "wgrad": wgrad, "part": part, "cpart": cpart,
    }
    forward(s)
    entropy(s, hw_ref, pw_ref)
    backward(s, hw_ref)

    core, x, y, z = place.core, place.x, place.y, place.z
    c1 = jnp.where(core == 0, x, y)
    c2 = jnp.where(core == 0, y, x)
    sibling = place.sibling()

    def pair_of(d):
        return (4 - d) % 4

    at = lambda ref, *index: ref.at[index]
    groups = part.reshape(2, 4, 4, 4, 16, 128)
    totals = total.reshape(2, 4, 4, 4, 16, 128)

    def go(copies):
        for copy in copies:
            copy.start()
        sends.extend(copies)
        for copy in copies:
            copy.wait_recv()

    go([
        remote(groups.at[1 - core], r1, as_.at[0], ar.at[0], sibling),
        remote(cpart.at[1 - core], q1, cs.at[0], cr.at[0], sibling),
    ])
    groups[core] = groups[core] + r1[...]
    cpart[core] = cpart[core] + q1[...]
    go(
        [
            remote(
                groups.at[core, (c1 + d) % 4], r2.at[d - 1], as_.at[d], ar.at[d],
                place.along_first(d),
            )
            for d in (1, 2, 3)
        ]
        + [
            remote(
                cpart.at[core, (z + d) % 4], q2.at[d - 1], cs.at[d], cr.at[d], place.along_z(d)
            )
            for d in (1, 2, 3)
        ]
    )
    groups[core, c1] = (groups[core, c1] + r2[0]) + (r2[1] + r2[2])
    cpart[core, z] = (cpart[core, z] + q2[0]) + (q2[1] + q2[2])
    go(
        [
            remote(
                groups.at[core, c1, (c2 + d) % 4], r3.at[d - 1], as_.at[3 + d], ar.at[3 + d],
                place.along_second(d),
            )
            for d in (1, 2, 3)
        ]
        + [
            remote(
                cpart.at[core, z, (y + d) % 4], q3.at[d - 1], cs.at[3 + d], cr.at[3 + d],
                place.along_y(d),
            )
            for d in (1, 2, 3)
        ]
    )
    groups[core, c1, c2] = (groups[core, c1, c2] + r3[0]) + (r3[1] + r3[2])
    cpart[core, z, y] = (cpart[core, z, y] + q3[0]) + (q3[1] + q3[2])
    go(
        [
            remote(
                groups.at[core, c1, c2, (z + d) % 4], r4.at[d - 1], as_.at[6 + d], ar.at[6 + d],
                place.along_z(d),
            )
            for d in (1, 2, 3)
        ]
        + [
            remote(
                cpart.at[core, z, y], q4.at[d - 1], cs.at[6 + d], cr.at[6 + d], place.along_x(d)
            )
            for d in (1, 2, 3)
        ]
    )
    totals[core, c1, c2, z] = (groups[core, c1, c2, z] + r4[0]) + (r4[1] + r4[2])
    block = (cpart[core, z, y] + q4[0]) + (q4[1] + q4[2])
    cg_ref[...] = pltpu.roll(block, (128 - 27 * x) % 128, 1)[:, 0:27]

    def gather(view, stage, along, received):
        copies = [
            remote(view, view, as_.at[stage + d], ar.at[stage + d], along(d)) for d in (1, 2, 3)
        ]
        for copy in copies:
            copy.start()
        sends.extend(copies)
        for d in (1, 2, 3):
            remote(
                view, received((4 - d) % 4), as_.at[stage + d], ar.at[stage + d], along(d)
            ).wait_recv()

    gather(
        totals.at[core, c1, c2, z], 9, place.along_z, lambda d: totals.at[core, c1, c2, (z + d) % 4]
    )
    gather(totals.at[core, c1, c2], 12, place.along_second, lambda d: totals.at[core, c1, (c2 + d) % 4])
    gather(totals.at[core, c1], 15, place.along_first, lambda d: totals.at[core, (c1 + d) % 4])
    last = remote(totals.at[core], totals.at[core], as_.at[19], ar.at[19], sibling)
    last.start()
    sends.append(last)
    remote(
        totals.at[core], totals.at[1 - core], as_.at[19], ar.at[19], sibling
    ).wait_recv()

    for half in range(2):
        pwg_ref[:, 128 * half : 128 * half + 128] = total[40 * half : 40 * half + 40].reshape(
            640, 128
        )
    for k in range(5):
        hwg_ref[:, 128 * k : 128 * k + 128] = total[80 + 8 * k : 88 + 8 * k].reshape(128, 128)
        hbg_ref[:, 128 * k : 128 * k + 128] = total[120, k : k + 1, :]
    for k in range(2):
        pbg_ref[:, 128 * k : 128 * k + 128] = total[120, 5 + k : 6 + k, :]
    for copy in sends:
        copy.wait_send()


def on_device(x, cw, gamma, beta, hw, hb, pw, pb):
    wl = jnp.pad(cw.reshape(32, 1728), ((0, 0), (0, 64)))
    gb = jnp.concatenate(
        [gamma, jnp.zeros((32, 32), F32), jnp.broadcast_to(beta[:, None], (32, 64))], axis=1
    )
    vmem = pltpu.VMEM
    scratch = [
        vmem((16, 4, 32, 128), BF),
        vmem((32, 128), BF),
        vmem((2, 2, 2, 32, 128), BF),
        vmem((10, 4, 2, 32, 128), BF),
        vmem((2, 32, 1792), BF),
        vmem((2, 32, 128), F32),
        vmem((64, 128), F32),
        vmem((1024, 1024), BF),
        vmem((3, 256, 1024), BF),
        vmem((2, 256, 256), F32),
        vmem((2, 256, 256), F32),
        vmem((256, 256), F32),
        vmem((640, 128), BF),
        vmem((256, 640), BF),
        vmem((640, 128), F32),
        vmem((256, 128), F32),
        vmem((256, 1024), F32),
        vmem((256, 1024), F32),
        vmem((256, 1024), BF),
        vmem((640, 1024), BF),
        vmem((640, 1024), F32),
        vmem((256, 1024), BF),
        vmem((128, 1024), BF),
        vmem((640, 1024), BF),
        vmem((256, 1024), BF),
        vmem((3, 256, 1024), F32),
        vmem((64, 2048), F32),
        vmem((128, 16, 128), F32),
        vmem((2, 4, 4, 32, 128), F32),
        vmem((128, 16, 128), F32),
        vmem((4, 4, 4, 16, 128), F32),
        vmem((3, 4, 4, 16, 128), F32),
        vmem((3, 4, 16, 128), F32),
        vmem((3, 16, 128), F32),
        vmem((4, 4, 32, 128), F32),
        vmem((3, 4, 32, 128), F32),
        vmem((3, 32, 128), F32),
        vmem((3, 32, 128), F32),
        pltpu.SemaphoreType.DMA((3,)),
        pltpu.SemaphoreType.DMA((13,)),
        pltpu.SemaphoreType.DMA((13,)),
        pltpu.SemaphoreType.DMA((20,)),
        pltpu.SemaphoreType.DMA((20,)),
        pltpu.SemaphoreType.DMA((10,)),
        pltpu.SemaphoreType.DMA((10,)),
    ]
    spec = pl.BlockSpec(memory_space=pltpu.VMEM)
    cg, hwg, hbg, pwg, pbg = pl.pallas_call(
        body,
        out_shape=(
            jax.ShapeDtypeStruct((32, 27), F32),
            jax.ShapeDtypeStruct((128, 640), F32),
            jax.ShapeDtypeStruct((1, 640), F32),
            jax.ShapeDtypeStruct((640, 256), F32),
            jax.ShapeDtypeStruct((1, 256), F32),
        ),
        in_specs=[spec] * 7,
        out_specs=(spec,) * 5,
        scratch_shapes=scratch,
        compiler_params=pltpu.CompilerParams(
            collective_id=0, has_side_effects=True, vmem_limit_bytes=56 * 1024 * 1024
        ),
    )(x, wl, gb, hw, hb.reshape(1, 640), pw, pb.reshape(1, 256))
    return cg, hwg, hbg.reshape(640), pwg, pbg.reshape(256)


def solution(mesh):
    placed = (
        P(None, "ch", "lat", "lon"),
        P("ch", None, None),
        P("ch", None),
        P("ch"),
        P(),
        P(),
        P(),
        P(),
    )
    return jax.shard_map(
        on_device,
        mesh=mesh,
        in_specs=placed,
        out_specs=(P("ch", ("lon", "lat")), P(), P(), P(), P()),
        check_vma=False,
    )
```

time: 819 us -> 79.3 us (0.10)
  waiting for transfers between devices: 641 us -> 0 us
  Pallas kernels: 0 us -> 68.5 us
  blocking collectives: 65.1 us -> 0 us
  local copies, waits for them, and re-layouts: 43.8 us -> 7.68 us
  matrix products: 33.1 us -> 0 us
  starting transfers between devices: 16.8 us -> 0 us
  between operations: 15.1 us -> 0.67 us
    unnamed x4 -> x0, waiting for transfers between devices: 427 us -> none
    psum x1 -> x0, waiting for transfers between devices: 152 us -> none  [on_device(): lax.psum((grads[0], grads[1], grads[2], grads[3]), ('lon', 'lat', 'ch'))]
    pallas_call x0 -> x1, Pallas kernels: none -> 68.5 us  [on_device(): pl.pallas_call(body, out_shape=(jax.ShapeDtypeStruct((32, 27), F32), jax....]
    psum x1 -> x0, blocking collectives: 65.1 us -> none  [on_device(): lax.psum((grads[0], grads[1], grads[2], grads[3]), ('lon', 'lat', 'ch'))]
    all_gather x1 -> x0, waiting for transfers between devices: 43.4 us -> none  [on_device(): gathered = lax.all_gather(padded, 'ch', axis=1, tiled=True)]
    dot_general x62 -> x0, matrix products: 33.1 us -> none  [the longest x27 13.2 us: convolve(): jnp.einsum('oc,lcab->loab', weight[:, offset, :], window, preferred_eleme...]
    slice x4 -> x0, local copies, waits for them, and re-layouts: 13.7 us -> none  [the longest x2 13.5 us: convolve(): source[lev_off:lev_off + levels, :, lat_off:lat_off + rows, lon_off:lon_o...]
    all_to_all x2 -> x0, starting transfers between devices: 11 us -> none  [the longest x1 5.64 us: on_device(): lax.all_to_all(pieces, ('lon', 'ch'), split_axis=0, concat_axis=0, tiled=...]
  transfers between devices with their start and end apart: 9 -> 0, of which waited for: 8 -> 0; matrix products, arithmetic and copies ran while one was open for 2% -> 0% of each run, Pallas kernels for 0% -> 0%
where the time goes in v1:
time: 79.3 us; the launch traced here: 78.9 us
  Pallas kernels  68.5 us (86%)
  local copies, waits for them, and re-layouts  7.68 us (10%)
  other arithmetic  2.03 us (3%)
    pallas_call x1, Pallas kernels, on_device(): pl.pallas_call(body, out_shape=(jax.ShapeDtypeStruct((32, 27), F32), jax....  68.5 us
    unnamed x15, local copies, waits for them, and re-layouts  6.06 us

profile of v1, /device:TPU:1, one launch (start us, length us, event | category | flops | bytes accessed | tf_op | source)
XLA Modules:
  0.0 78.9 jit_solution(2547640070608346310)
XLA Ops:
  0.6 1.0 %copy.14 = bf16[32,27,64]{2,1,0:T(8,128)(2,1)S(1)} copy(bf16[32,27,64]{2,0,1:T(8,128)(2,1)} %param.9) | data formatting | bytes 221184 | tf_op args[1]
  1.7 0.2 reshape.26
  1.9 0.0 copy-start.4
  1.9 0.7 pad.4.wl_ref
  2.6 0.0 copy-done.4
  2.6 0.0 copy-start.1
  2.6 0.1 broadcast_in_dim.10
  2.7 0.1 pad.6.clone
  2.7 0.6 copy-done.1
  3.3 0.0 copy-start.2
  3.3 0.7 pad_maximum_fusion.gb_ref
  4.0 0.0 copy-done.2
  4.0 0.6 reshape.27.hb_ref
  4.6 68.5 %shard_map.119 = (f32[32,27]{1,0:T(8,128)}, f32[128,640]{1,0:T(8,128)}, f32[1,640]{1,0:T(1,128)}, f32[640,256]{1,0:T(8,128)}, f32[1,256]{1,0:T(1,128)}) custom-call(bf16[4,32,16,128]{3,2,1,0:T(8,128)(2,1)} %x_ref.1, bf16[32,1792]{1,0:T(8,128)(2,1)} %pad.4.wl_ref, f32[32,128]{1,0:T(8,128)} %pad_maximum_fusion.gb_ref, bf16[128,640]{1,0:T(8,128)(2,1)} %hw_ref.1, ...), custom_call_target="tpu_custom_call" | custom-call | tf_op jit(solution)/shard_map/pallas_call | solution.py:637
  73.1 0.0 copy-start
  73.1 1.3 %reduce = f32[640]{0:T(1024)} reduce(f32[1,640]{1,0:T(1,128)} %get-tuple-element.12, f32[]{:T(128)} %constant.7), dimensions={0}, to_apply=%get-tuple-element.12.reduce_sub_computation | reduce | bytes 5124 | tf_op jit(solution)/shard_map/pallas_call | solution.py:637
  74.5 1.3 %copy.19 = f32[32,27]{1,0:T(8,128)} copy(f32[32,27]{1,0:T(8,128)} %get-tuple-element.20) | data formatting | bytes 6912
  75.8 1.7 %copy.20 = f32[128,640]{1,0:T(8,128)} copy(f32[128,640]{1,0:T(8,128)} %get-tuple-element.21) | data formatting | bytes 655360
  77.5 0.0 copy-done
  77.5 0.0 copy-start.3
  77.5 0.8 %copy.21 = f32[640,256]{1,0:T(8,128)} copy(f32[640,256]{1,0:T(8,128)S(1)} %copy-done) | data formatting | bytes 1310720
  78.4 0.0 copy-done.3
  78.4 0.6 copy.22
  (1 shorter events, 0.0 us)
Async XLA Ops:
  1.9 0.7 copy-start.4
  2.6 0.7 copy-start.1
  3.3 0.7 copy-start.2
  73.1 4.4 %copy-start = (f32[640,256]{1,0:T(8,128)S(1)}, f32[640,256]{1,0:T(8,128)}, u32[]{:S(2)}) copy-start(f32[640,256]{1,0:T(8,128)} %get-tuple-element.23) | copy-start | bytes 1966084
  77.5 0.8 %copy-start.3 = (f32[1,256]{1,0:T(1,128)S(1)}, f32[1,256]{1,0:T(1,128)}, u32[]{:S(2)}) copy-start(f32[1,256]{1,0:T(1,128)} %get-tuple-element.14) | copy-start | bytes 3076

commit v2 on v1

v2 whole, which is shorter than its diff:
```python
import jax
import jax.numpy as jnp
from jax import lax
from jax.experimental import pallas as pl
from jax.experimental.pallas import tpu as pltpu
from jax.sharding import PartitionSpec as P

BF = jnp.bfloat16
F32 = jnp.float32
MESH = pl.DeviceIdType.MESH
PATCHES = 131072.0

NN = (((1,), (0,)), ((), ()))
NT = (((1,), (1,)), ((), ()))


def mm(a, b, dims=NN):
    return lax.dot_general(a, b, dims, preferred_element_type=F32)


def iota(shape, dim):
    return lax.broadcasted_iota(jnp.int32, shape, dim)


def onehot(condition):
    return jnp.where(condition, 1.0, 0.0).astype(BF)


def split(value):
    high = value.astype(BF)
    return high, (value - high.astype(F32)).astype(BF)


class Place:
    def __init__(self):
        self.lon = lax.axis_index("lon")
        self.lat = lax.axis_index("lat")
        self.ch = lax.axis_index("ch")
        self.core = self.lon % 2
        self.y = (self.lon // 2) % 4
        self.zlo = self.lon // 8
        self.x = self.lat
        self.z = self.ch * 2 + self.zlo
        self.c1 = jnp.where(self.core == 0, self.x, self.y)
        self.c2 = jnp.where(self.core == 0, self.y, self.x)

    def chip(self, x, y, z, core):
        return ((z % 2) * 8 + y * 2 + core, x, z // 2)

    def sibling(self):
        return self.chip(self.x, self.y, self.z, 1 - self.core)

    def along_x(self, d):
        return self.chip((self.x + d) % 4, self.y, self.z, self.core)

    def along_y(self, d):
        return self.chip(self.x, (self.y + d) % 4, self.z, self.core)

    def along_z(self, d):
        return self.chip(self.x, self.y, (self.z + d) % 4, self.core)

    def along_first(self, d):
        on_x = 1 - self.core
        return self.chip(
            (self.x + d * on_x) % 4, (self.y + d * (1 - on_x)) % 4, self.z, self.core
        )

    def in_plane(self, c2, z):
        x = jnp.where(self.core == 0, self.x, c2)
        y = jnp.where(self.core == 0, c2, self.y)
        return self.chip(x, y, z, self.core)


def remote(src, dst, send, recv, device):
    return pltpu.make_async_remote_copy(
        src_ref=src,
        dst_ref=dst,
        send_sem=send,
        recv_sem=recv,
        device_id=device,
        device_id_type=MESH,
    )


def enter(place):
    lon, lat, ch = place.lon, place.lat, place.ch
    barrier = pltpu.get_barrier_semaphore()
    row = (lat + 2 * ch + 3) % 4
    devices = [(lon, lat, 1 - ch), (lon, row, 0), (lon, row, 1)]
    for side in (1, 15):
        for other in (0, 1):
            devices.append(((lon + side) % 16, lat, other))
            devices.append(((lon + side) % 16, row, other))
    devices.append(place.sibling())
    for d in (1, 2, 3):
        devices += [place.along_x(d), place.along_y(d), place.along_z(d)]
    for a in range(1, 4):
        for d in range(1, 4):
            devices.append(place.in_plane((place.c2 + a) % 4, (place.z + d) % 4))
    for device in devices:
        pl.semaphore_signal(barrier, inc=1, device_id=device, device_id_type=MESH)
    return barrier, len(devices)


def shuffle_latents(x_ref, own, rim_out):
    rows, cols = iota((512, 512), 0), iota((512, 512), 1)
    swap = onehot(cols == (rows % 32) * 16 + rows // 32)
    b, n = iota((128, 256), 0), iota((128, 256), 1)
    parity = jnp.where(n < 64, 2 * n, 2 * (n - 64) + 1)
    edge = jnp.where(n < 192, 0, 127)
    spread = onehot(b == jnp.where(n < 128, parity, edge))
    r, j = iota((512, 128), 0), iota((512, 128), 1)
    rims = jnp.zeros((512, 128), F32)
    for level in range(4):
        block = mm(x_ref[level].reshape(512, 128), spread)
        rims = jnp.where((j % 64) == (r % 16) * 4 + level, block[:, 128:], rims)
        own[level] = mm(swap, block[:, :128].astype(BF)).astype(BF).reshape(16, 32, 128)
    c, k = iota((32, 512), 0), iota((32, 512), 1)
    rim_out[...] = mm(onehot(k // 16 == c), rims.astype(BF)).astype(BF)


def pack_weights(cw_ref, gamma_ref, beta_ref, wl, gb):
    for k in range(13):
        wl[:, 128 * k : 128 * k + 128] = jnp.concatenate(
            [cw_ref[2 * k].astype(F32), cw_ref[2 * k + 1].astype(F32)], axis=1
        ).astype(BF)
    wl[:, 1664:1792] = jnp.concatenate(
        [cw_ref[26].astype(F32), jnp.zeros((32, 64), F32)], axis=1
    ).astype(BF)
    line = beta_ref[...].reshape(1, 32)
    column = jnp.sum(
        jnp.where(iota((32, 32), 0) == iota((32, 32), 1), line, 0.0), axis=1, keepdims=True
    )
    gb[:, 0:32] = gamma_ref[...]
    gb[:, 32:128] = jnp.broadcast_to(column, (32, 96))


def prepare_small(hw, hb_ref, pw, pb_ref, hwt, pwt, hbt, pbt):
    eye = onehot(iota((128, 128), 0) == iota((128, 128), 1))
    for k in range(5):
        part = slice(128 * k, 128 * k + 128)
        hwt[part, :] = mm(eye, hw[:, part], NT).astype(BF)
        hbt[part, :] = jnp.broadcast_to(hb_ref[part].reshape(1, 128), (128, 128)).T
    for k in range(2):
        part = slice(128 * k, 128 * k + 128)
        pwt[part, :] = mm(eye, pw[:, part], NT).astype(BF)
        pbt[part, :] = jnp.broadcast_to(pb_ref[part].reshape(1, 128), (128, 128)).T


def build_gamma(gall, gam, gamt, beta):
    k, n = iota((128, 256), 0), iota((128, 256), 1)
    copies = onehot(k == n % 32)
    for g in range(2):
        high, low = split(gall[g])
        for which, part in ((0, high), (1, low)):
            wide = mm(part, copies)
            for s in range(4):
                block = g * 4 + s
                own_block = iota((32, 256), 1) // 32 == block
                gam[which, block * 32 : block * 32 + 32, :] = jnp.where(own_block, wide, 0.0)
        for s in range(4):
            block = g * 4 + s
            beta[block * 32 : block * 32 + 32, :] = jnp.broadcast_to(
                gall[g][:, 64:65], (32, 256)
            )
    for which in range(2):
        gamt[which] = gam[which].T


def build_weights(wall, wf):
    lane = iota((32, 256), 1)
    for g in range(2):
        for n in range(9):
            dl, da = n // 3, n % 3
            base = (192 * n) // 128 * 128
            v = wall[g, :, base : base + 256].astype(F32)
            first = v if n % 2 == 0 else pltpu.roll(v, 192, 1)
            second = v if n % 2 == 1 else pltpu.roll(v, 64, 1)
            first = jnp.where(lane < 192, first, 0.0).astype(BF)
            second = jnp.where(lane >= 64, second, 0.0).astype(BF)
            for p in range(2):
                r = da + p
                row = g * 128 + 2 * p * 32
                wf[dl, row : row + 32, 256 * r : 256 * r + 256] = first
                wf[dl, row + 32 : row + 64, 256 * r : 256 * r + 256] = second
        for dl in range(3):
            for p in range(2):
                r = 3 if p == 0 else 0
                row = g * 128 + 2 * p * 32
                wf[dl, row : row + 64, 256 * r : 256 * r + 256] = jnp.zeros((64, 256), BF)


def place_rims(place, rim_in, rims):
    chi, lat = place.ch, place.lat
    k, n = iota((512, 128), 0), iota((512, 128), 1)
    block, kk, nn = k // 128, k % 128, n % 64
    left = block < 2
    same = block % 2 == 0
    pole = jnp.where(chi == 0, lat, 3 - lat) == 0
    shift_same = (8 * chi - 1) * 4
    other_low = 36 * chi
    shift_other = jnp.where(chi == 0, 60, -36)
    shift = jnp.where(same, shift_same, shift_other)
    source = nn + shift
    inside = (source >= 0) & (source < 64) & (nn < 40)
    only = (nn >= other_low) & (nn < other_low + 4) & jnp.logical_not(pole)
    valid = inside & (same | only)
    side = (left & (n < 64)) | (jnp.logical_not(left) & (n >= 64))
    chosen = kk == source + jnp.where(left, 64, 0)
    pick = onehot(valid & side & chosen)
    tiles = jnp.concatenate(
        [rim_in[s, t].reshape(64, 128) for s in range(2) for t in range(2)], axis=1
    )
    rims[...] = mm(tiles, pick)


def window_pick():
    col = iota((1, 512), 1)
    w, js, m = col // 128, (col % 128) // 64, col % 64
    target = jnp.where(
        w == 0,
        jnp.where(m == 0, 256 + js * 8, js * 128 + 63 + m),
        jnp.where(
            w == 1,
            js * 128 + m,
            jnp.where(
                w == 2,
                js * 128 + 64 + m,
                jnp.where(m == 63, 320 + js * 8, js * 128 + m + 1),
            ),
        ),
    )
    return onehot(iota((384, 512), 0) == target)


def build_windows(field, rims, pick, xt, level):
    stack = []
    for r in range(4):
        for pair in range(2):
            j0 = r + 4 * pair
            edge = pltpu.roll(rims[...], 128 - (j0 * 4 + level), 1).astype(BF)
            rows = [field[level, :, j].reshape(64, 128) for j in (j0, j0 + 2)]
            stack.append(jnp.concatenate(rows + [edge], axis=1))
    out = mm(jnp.concatenate(stack, axis=0), pick[...]).astype(BF)
    for r in range(4):
        for pair in range(2):
            row, lane = (r * 2 + pair) * 64, level * 256 + pair * 128
            for v in range(4):
                xt[r * 256 + v * 64 : r * 256 + v * 64 + 64, lane : lane + 128] = out[
                    row : row + 64, v * 128 : v * 128 + 128
                ]


def mix(gam, value):
    high, low = split(value)
    ghigh, glow = gam[0].astype(BF), gam[1].astype(BF)
    return mm(ghigh, high) + (mm(ghigh, low) + mm(glow, high))


def forward(s, level):
    lanes = slice(256 * level, 256 * level + 256)
    total = None
    for dl in range(3):
        other = level + dl - 1
        if 0 <= other < 4:
            term = mm(s["wf"][dl], s["xt"][:, 256 * other : 256 * other + 256])
            total = term if total is None else total + term
    s["conv"][:, lanes] = total
    inv = lax.rsqrt(s["beta"][...] + mix(s["gam"], total * total))
    s["inv"][:, lanes] = inv
    s["normed"][:, lanes] = (total * inv).astype(BF)


def entropy_forward(s):
    def first(i, carry):
        lanes = pl.ds(pl.multiple_of(i * 256, 256), 256)
        features = s["normed"][0:128, lanes]
        for k in range(5):
            part = slice(128 * k, 128 * k + 128)
            bias = s["hbt"][part, :]
            pre = mm(s["hwt"][part, :], features) + jnp.concatenate([bias, bias], axis=1)
            sig = 1.0 / (1.0 + jnp.exp(-pre))
            act = pre * sig
            s["hidden"][part, lanes] = act.astype(BF)
            s["gate"][part, lanes] = sig * (1.0 + pre - act)
        return carry

    lax.fori_loop(0, 4, first, 0)

    def second(i, carry):
        lanes = pl.ds(pl.multiple_of(i * 256, 256), 256)
        hidden = s["hidden"][:, lanes]
        cb, rb = s["pbt"][0:128, :], s["pbt"][128:256, :]
        centre = mm(s["pwt"][0:128, :], hidden) + jnp.concatenate([cb, cb], axis=1)
        raw = mm(s["pwt"][128:256, :], hidden) + jnp.concatenate([rb, rb], axis=1)
        small = jnp.exp(-jnp.abs(raw))
        spread = 0.5 + jnp.maximum(raw, 0.0) + jnp.log1p(small)
        sig = jnp.where(raw >= 0.0, 1.0, small) / (1.0 + small)
        over = 1.0 / spread
        error = (s["normed"][128:256, lanes].astype(F32) - centre) * over
        ratio = error * over * (1.0 / PATCHES)
        s["dparams"][0:128, lanes] = (-ratio).astype(BF)
        s["dparams"][128:256, lanes] = (
            (1.0 - error * error) * over * sig * (1.0 / PATCHES)
        ).astype(BF)
        s["dtargets"][:, lanes] = ratio.astype(BF)
        return carry

    lax.fori_loop(0, 4, second, 0)

    grad = mm(s["hidden"][...], s["dparams"][...], NT)
    for half in range(2):
        for k in range(4):
            s["part"][half, k, 0:10] = grad[
                160 * k : 160 * k + 160, 128 * half : 128 * half + 128
            ].reshape(10, 16, 128)


def entropy_backward(s, pw):
    def third(i, carry):
        lanes = pl.ds(pl.multiple_of(i * 256, 256), 256)
        back = mm(pw[...], s["dparams"][:, lanes])
        s["dpre"][:, lanes] = (back * s["gate"][:, lanes]).astype(BF)
        return carry

    lax.fori_loop(0, 4, third, 0)


def hidden_grads(s):
    part = s["part"]
    ones = jnp.ones((8, 1024), BF)
    pb = mm(ones, s["dparams"][...], NT)
    grad = mm(s["normed"][0:128, :], s["dpre"][...], NT)
    for k in range(5):
        for n in range(8):
            part[n // 4, n % 4, 10 + k] = grad[16 * n : 16 * n + 16, 128 * k : 128 * k + 128]
    hb = mm(ones, s["dpre"][...], NT)
    zeros = jnp.zeros((1, 128), F32)
    lines = [hb[0:1, 128 * k : 128 * k + 128] for k in range(5)]
    lines += [pb[0:1, 0:128], pb[0:1, 128:256]] + [zeros] * 9
    for n in range(8):
        part[n // 4, n % 4, 15] = jnp.zeros((16, 128), F32)
    part[0, 0, 15] = jnp.concatenate(lines, axis=0)


def conv_backward(s, hw):
    for level in range(4):
        lanes = slice(256 * level, 256 * level + 256)
        dfeat = mm(hw[...], s["dpre"][:, lanes]).astype(BF).astype(F32)
        dn = jnp.concatenate([dfeat, s["dtargets"][:, lanes].astype(F32)], axis=0)
        inv = s["inv"][:, lanes]
        y = s["conv"][:, lanes]
        dni = dn * inv
        weighted = dni * y * (inv * inv)
        s["dconv"][:, lanes] = (dni - y * mix(s["gamt"], weighted)).astype(BF)


def weight_grads(s):
    for dl in range(3):
        first, last = max(0, 1 - dl), min(4, 5 - dl)
        d = s["dconv"][:, 256 * first : 256 * last]
        x = s["xt"][:, 256 * (first + dl - 1) : 256 * (last + dl - 1)]
        s["taps"][dl] = mm(d, x, NT)
    for dl in range(3):
        for da in range(3):
            n = dl * 3 + da
            for g in range(2):
                total = None
                for p in range(2):
                    row = g * 128 + 2 * p * 32
                    lanes = slice(256 * (da + p), 256 * (da + p) + 256)
                    a = s["taps"][dl, row : row + 32, lanes]
                    b = s["taps"][dl, row + 32 : row + 64, lanes]
                    term = a + pltpu.roll(b, 192, 1)
                    total = term if total is None else total + term
                s["wgrad"][32 * g : 32 * g + 32, 192 * n : 192 * n + 192] = total[:, 0:192]
    s["wgrad"][:, 1728:2048] = jnp.zeros((64, 320), F32)
    for k in range(16):
        start = 108 * k
        base = start // 128 * 128
        shift = (256 - (start - base)) % 256
        v = s["wgrad"][:, base : base + 256]
        v = pltpu.roll(v, shift, 1)[:, 0:128] if shift else v[:, 0:128]
        core, y, zlo = k % 2, (k // 2) % 4, k // 8
        for g in range(2):
            s["cpart"][core, g * 2 + zlo, y] = v[32 * g : 32 * g + 32, :]


def body(
    x_hbm, cw_hbm, gamma_ref, beta_ref, hw_hbm, hb_ref, pw_hbm, pb_ref,
    total_ref, cg_ref,
    x, cw, hw, pw, wl, gb,
    own, rim_out, rim_in, field, wall, gall, rims, pick,
    xt, wf, gam, gamt, beta, hwt, pwt, hbt, pbt,
    conv, inv, normed, hidden, gate, dparams, dtargets, dpre, dconv, taps, wgrad,
    part, cpart, r1, r2, r3, q1, q2, q3, q4,
    local_sem, xs, xr, as_, ar, bs, br, gs, gr, cs, cr,
):
    place = Place()
    lon, lat, chi = place.lon, place.lat, place.ch
    core, c1, c2, z, y = place.core, place.c1, place.c2, place.z, place.y
    partner = (lon, lat, 1 - chi)
    sibling = place.sibling()
    other = 1 - chi
    loads = [
        pltpu.make_async_copy(src, dst, local_sem.at[n])
        for n, (src, dst) in enumerate(((x_hbm, x), (cw_hbm, cw), (hw_hbm, hw), (pw_hbm, pw)))
    ]
    for copy in loads:
        copy.start()
    barrier, count = enter(place)
    loads[1].wait()
    pack_weights(cw, gamma_ref, beta_ref, wl, gb)
    loads[0].wait()
    shuffle_latents(x, own, rim_out)
    pl.semaphore_wait(barrier, count)

    mine = pl.ds(pl.multiple_of(16 * core, 16), 16)
    theirs = pl.ds(pl.multiple_of(16 * (1 - core), 16), 16)
    sends = []

    def start(*copies):
        for copy in copies:
            copy.start()
        sends.extend(copies)
        return copies

    def arrive(copies):
        for copy in copies:
            copy.wait_recv()

    start(
        remote(wl.at[mine], wall.at[chi, mine], xs.at[4], xr.at[4], partner),
        remote(gb, gall.at[chi], xs.at[5], xr.at[5], partner),
    )
    down, up = (lat + 3) % 4, (lat + 1) % 4
    for side in range(2):
        near = (lon + 1) % 16 if side == 0 else (lon + 15) % 16
        for kind, (row, half) in enumerate(((lat, 0), (lat, 1), (down, 1), (up, 0))):
            slot = 9 + (side * 2 + kind // 2) * 2
            start(
                remote(
                    rim_out, rim_in.at[side, kind // 2, chi],
                    xs.at[9 + side * 4 + kind], xr.at[slot + chi], (near, row, half),
                )
            )
    start(
        remote(own.at[:, 0], field.at[:, chi, 9], xs.at[7], xr.at[7 + chi], (lon, down, 1)),
        remote(own.at[:, 15], field.at[:, chi, 0], xs.at[8], xr.at[7 + chi], (lon, up, 0)),
    )
    for level in range(4):
        start(
            remote(
                own.at[level, pl.ds(7 * other, 9)], field.at[level, chi, pl.ds(chi, 9)],
                xs.at[level], xr.at[level], partner,
            )
        )
    for level in range(4):
        field[level, chi, pl.ds(other, 9)] = own[level, pl.ds(7 * chi, 9)]
    wall[chi] = wl[...]
    gall[chi] = gb[...]
    loads[2].wait()
    loads[3].wait()
    prepare_small(hw, hb_ref, pw, pb_ref, hwt, pwt, hbt, pbt)
    pick[...] = window_pick()
    remote(gb, gall.at[other], xs.at[5], xr.at[5], partner).wait_recv()
    remote(wl.at[mine], wall.at[other, mine], xs.at[4], xr.at[4], partner).wait_recv()
    start(remote(wall.at[other, mine], wall.at[other, mine], xs.at[6], xr.at[6], sibling))
    build_gamma(gall, gam, gamt, beta)
    for half in range(2):
        remote(
            own.at[:, 0], field.at[:, half, 9 * chi], xs.at[7], xr.at[7 + half], partner
        ).wait_recv()
    for side in range(2):
        for kind in range(2):
            for half in range(2):
                remote(
                    rim_out, rim_in.at[side, kind, half], xs.at[9],
                    xr.at[9 + (side * 2 + kind) * 2 + half], partner,
                ).wait_recv()
    place_rims(place, rim_in, rims)
    remote(
        wall.at[other, mine], wall.at[other, theirs], xs.at[6], xr.at[6], sibling
    ).wait_recv()
    build_weights(wall, wf)

    @pl.when(jnp.where(chi == 0, lat, 3 - lat) == 0)
    def _():
        field[:, :, pl.ds(9 * chi, 1)] = jnp.zeros((4, 2, 1, 32, 128), BF)

    s = {
        "xt": xt, "wf": wf, "gam": gam, "gamt": gamt, "beta": beta, "hwt": hwt, "pwt": pwt,
        "hbt": hbt, "pbt": pbt, "conv": conv, "inv": inv, "normed": normed, "hidden": hidden,
        "gate": gate, "dparams": dparams, "dtargets": dtargets, "dpre": dpre, "dconv": dconv,
        "taps": taps, "wgrad": wgrad, "part": part, "cpart": cpart,
    }
    for level in range(4):
        remote(
            own.at[level, pl.ds(0, 9)], field.at[level, other, pl.ds(other, 9)],
            xs.at[level], xr.at[level], partner,
        ).wait_recv()
        build_windows(field, rims, pick, xt, level)
        if level >= 1:
            forward(s, level - 1)
    forward(s, 3)
    entropy_forward(s)

    spans = (pl.ds(0, 10), pl.ds(10, 6))
    p = c2 * 4 + z

    def core_stage(n):
        return start(
            remote(part.at[1 - core, :, spans[n]], r1.at[:, spans[n]], as_.at[n], ar.at[n], sibling)
        )

    def core_add(n):
        part[core, :, spans[n]] = part[core, :, spans[n]] + r1[:, spans[n]]

    def axis_stage(n):
        return start(
            *[
                remote(
                    part.at[core, (c1 + d) % 4, spans[n]], r2.at[d - 1, spans[n]],
                    as_.at[1 + 3 * n + d], ar.at[1 + 3 * n + d], place.along_first(d),
                )
                for d in (1, 2, 3)
            ]
        )

    def axis_add(n):
        part[core, c1, spans[n]] = (part[core, c1, spans[n]] + r2[0, spans[n]]) + (
            r2[1, spans[n]] + r2[2, spans[n]]
        )

    owners = (range(0, 10), range(10, 16))

    def apart(o, act):
        pl.when(p != o)(act)

    def plane_copy(o):
        return remote(
            part.at[core, c1, o], r3.at[p], bs.at[o], br.at[p], place.in_plane(o // 4, o % 4)
        )

    def plane_stage(n):
        for o in owners[n]:
            apart(o, lambda o=o: plane_copy(o).start())

    def spread_copy(o):
        view = total_ref.at[core, c1, p]
        return remote(view, view, gs.at[o], gr.at[p], place.in_plane(o // 4, o % 4))

    def plane_finish(n):
        @pl.when((p < 10) if n == 0 else (p >= 10))
        def _():
            r3[p] = part[core, c1, p]
            for o in range(16):
                apart(
                    o,
                    lambda o=o: remote(
                        part.at[core, c1, o], r3.at[o], bs.at[o], br.at[o], sibling
                    ).wait_recv(),
                )
            terms = [r3[o] for o in range(16)]
            while len(terms) > 1:
                terms = [terms[k] + terms[k + 1] for k in range(0, len(terms), 2)]
            total_ref[core, c1, p] = terms[0]
            for o in range(16):
                apart(o, lambda o=o: spread_copy(o).start())

    def spread_finish(n):
        for o in owners[n]:
            apart(
                o,
                lambda o=o: remote(
                    part.at[core, c1, o], total_ref.at[core, c1, o], gs.at[o], gr.at[o], sibling
                ).wait_recv(),
            )

    def axis_spread(n):
        view = total_ref.at[core, c1, spans[n]]
        return start(
            *[
                remote(
                    view, view, as_.at[7 + 3 * n + d], ar.at[7 + 3 * n + d], place.along_first(d)
                )
                for d in (1, 2, 3)
            ]
        )

    def axis_arrive(n):
        for d in (1, 2, 3):
            remote(
                total_ref.at[core, c1, spans[n]],
                total_ref.at[core, (c1 + 4 - d) % 4, spans[n]],
                as_.at[7 + 3 * n + d], ar.at[7 + 3 * n + d], sibling,
            ).wait_recv()

    def core_spread(n):
        view = total_ref.at[core, :, spans[n]]
        start(remote(view, view, as_.at[14 + n], ar.at[14 + n], sibling))

    def core_arrive(n):
        remote(
            total_ref.at[core, :, spans[n]], total_ref.at[1 - core, :, spans[n]],
            as_.at[14 + n], ar.at[14 + n], sibling,
        ).wait_recv()

    going = core_stage(0)
    entropy_backward(s, pw)
    arrive(going)
    core_add(0)
    going_axis = axis_stage(0)
    hidden_grads(s)
    going = core_stage(1)
    conv_backward(s, hw)
    arrive(going)
    core_add(1)
    going_axis1 = axis_stage(1)
    weight_grads(s)
    going = start(remote(cpart.at[1 - core], q1, cs.at[0], cr.at[0], sibling))
    arrive(going_axis)
    axis_add(0)
    plane_stage(0)
    arrive(going)
    cpart[core] = cpart[core] + q1[...]
    going = start(
        *[
            remote(
                cpart.at[core, (z + d) % 4], q2.at[d - 1], cs.at[d], cr.at[d], place.along_z(d)
            )
            for d in (1, 2, 3)
        ]
    )
    arrive(going_axis1)
    axis_add(1)
    plane_stage(1)
    plane_finish(0)
    arrive(going)
    cpart[core, z] = (cpart[core, z] + q2[0]) + (q2[1] + q2[2])
    going = start(
        *[
            remote(
                cpart.at[core, z, (y + d) % 4], q3.at[d - 1], cs.at[3 + d], cr.at[3 + d],
                place.along_y(d),
            )
            for d in (1, 2, 3)
        ]
    )
    plane_finish(1)
    spread_finish(0)
    axis_spread(0)
    arrive(going)
    cpart[core, z, y] = (cpart[core, z, y] + q3[0]) + (q3[1] + q3[2])
    going = start(
        *[
            remote(
                cpart.at[core, z, y], q4.at[d - 1], cs.at[6 + d], cr.at[6 + d], place.along_x(d)
            )
            for d in (1, 2, 3)
        ]
    )
    spread_finish(1)
    axis_spread(1)
    axis_arrive(0)
    core_spread(0)
    arrive(going)
    block = (cpart[core, z, y] + q4[0]) + (q4[1] + q4[2])
    cg_ref[...] = pltpu.roll(block, (128 - 27 * place.x) % 128, 1)
    axis_arrive(1)
    core_spread(1)
    core_arrive(0)
    core_arrive(1)
    for copy in sends:
        copy.wait_send()
    for o in range(16):
        apart(o, lambda o=o: plane_copy(o).wait_send())
        apart(o, lambda o=o: spread_copy(o).wait_send())


def unpack(total_ref, block_ref, cg_ref, hwg_ref, hbg_ref, pwg_ref, pbg_ref):
    cg_ref[...] = block_ref[:, 0:27]
    for half in range(2):
        for k in range(4):
            pwg_ref[160 * k : 160 * k + 160, 128 * half : 128 * half + 128] = total_ref[
                half, k, 0:10
            ].reshape(160, 128)
    for n in range(8):
        for k in range(5):
            hwg_ref[16 * n : 16 * n + 16, 128 * k : 128 * k + 128] = total_ref[
                n // 4, n % 4, 10 + k
            ]
    for k in range(5):
        hbg_ref[128 * k : 128 * k + 128] = total_ref[0, 0, 15, k]
    for k in range(2):
        pbg_ref[128 * k : 128 * k + 128] = total_ref[0, 0, 15, 5 + k]


def on_device(x, cw, gamma, beta, hw, hb, pw, pb):
    vmem = pltpu.VMEM
    dma = pltpu.SemaphoreType.DMA
    scratch = [
        vmem((4, 32, 16, 128), BF),
        vmem((27, 32, 64), BF),
        vmem((128, 640), BF),
        vmem((640, 256), BF),
        vmem((32, 1792), BF),
        vmem((32, 128), F32),
        vmem((4, 16, 32, 128), BF),
        vmem((32, 128), BF),
        vmem((2, 2, 2, 32, 128), BF),
        vmem((4, 2, 10, 32, 128), BF),
        vmem((2, 32, 1792), BF),
        vmem((2, 32, 128), F32),
        vmem((64, 128), F32),
        vmem((384, 512), BF),
        vmem((1024, 1024), BF),
        vmem((3, 256, 1024), BF),
        vmem((2, 256, 256), F32),
        vmem((2, 256, 256), F32),
        vmem((256, 256), F32),
        vmem((640, 128), BF),
        vmem((256, 640), BF),
        vmem((640, 128), F32),
        vmem((256, 128), F32),
        vmem((256, 1024), F32),
        vmem((256, 1024), F32),
        vmem((256, 1024), BF),
        vmem((640, 1024), BF),
        vmem((640, 1024), F32),
        vmem((256, 1024), BF),
        vmem((128, 1024), BF),
        vmem((640, 1024), BF),
        vmem((256, 1024), BF),
        vmem((3, 256, 1024), F32),
        vmem((64, 2048), F32),
        vmem((2, 4, 16, 16, 128), F32),
        vmem((2, 4, 4, 32, 128), F32),
        vmem((4, 16, 16, 128), F32),
        vmem((3, 16, 16, 128), F32),
        vmem((16, 16, 128), F32),
        vmem((4, 4, 32, 128), F32),
        vmem((3, 4, 32, 128), F32),
        vmem((3, 32, 128), F32),
        vmem((3, 32, 128), F32),
        dma((4,)),
        dma((17,)),
        dma((17,)),
        dma((16,)),
        dma((16,)),
        dma((16,)),
        dma((16,)),
        dma((16,)),
        dma((16,)),
        dma((10,)),
        dma((10,)),
    ]
    spec = pl.BlockSpec(memory_space=pltpu.VMEM)
    anywhere = pl.BlockSpec(memory_space=pl.ANY)
    total, block = pl.pallas_call(
        body,
        out_shape=(
            jax.ShapeDtypeStruct((2, 4, 16, 16, 128), F32),
            jax.ShapeDtypeStruct((32, 128), F32),
        ),
        in_specs=[anywhere, anywhere, spec, spec, anywhere, spec, anywhere, spec],
        out_specs=(spec, spec),
        scratch_shapes=scratch,
        compiler_params=pltpu.CompilerParams(
            collective_id=0, has_side_effects=True, vmem_limit_bytes=56 * 1024 * 1024
        ),
    )(x, jnp.transpose(cw, (1, 0, 2)), gamma, beta, hw, hb, pw, pb)
    return pl.pallas_call(
        unpack,
        out_shape=(
            jax.ShapeDtypeStruct((32, 27), F32),
            jax.ShapeDtypeStruct((128, 640), F32),
            jax.ShapeDtypeStruct((640,), F32),
            jax.ShapeDtypeStruct((640, 256), F32),
            jax.ShapeDtypeStruct((256,), F32),
        ),
        in_specs=[spec] * 2,
        out_specs=(spec,) * 5,
    )(total, block)


def solution(mesh):
    placed = (
        P(None, "ch", "lat", "lon"),
        P("ch", None, None),
        P("ch", None),
        P("ch"),
        P(),
        P(),
        P(),
        P(),
    )
    return jax.shard_map(
        on_device,
        mesh=mesh,
        in_specs=placed,
        out_specs=(P("ch", ("lon", "lat")), P(), P(), P(), P()),
        check_vma=False,
    )
```

time: 79.3 us -> 58.1 us (0.73)
  Pallas kernels: 68.5 us -> 57.3 us
  local copies, waits for them, and re-layouts: 7.68 us -> 0 us
  other arithmetic: 2.03 us -> 0 us
    pallas_call x1 -> x2, Pallas kernels: 68.5 us -> 57.3 us  [the longest x1 55.1 us: on_device(): pl.pallas_call(body, out_shape=(jax.ShapeDtypeStruct((2, 4, 16, 16, 128),...]
    unnamed x15 -> x0, local copies, waits for them, and re-layouts: 6.06 us -> none
    pallas_call x1 -> x0, other arithmetic: 1.35 us -> none  [on_device(): pl.pallas_call(body, out_shape=(jax.ShapeDtypeStruct((32, 27), F32), jax....]
    reshape x2 -> x0, local copies, waits for them, and re-layouts: 0.82 us -> none  [the longest x1 0.58 us: on_device(): hb.reshape(1, 640)]
where the time goes in v2:
time: 58.1 us; the launch traced here: 57.9 us
  Pallas kernels  57.3 us (99%)
  between operations  0.64 us (1%)
    pallas_call x1, Pallas kernels, on_device(): pl.pallas_call(body, out_shape=(jax.ShapeDtypeStruct((2, 4, 16, 16, 128),...  55.1 us
    pallas_call x1, Pallas kernels, on_device(): pl.pallas_call(unpack, out_shape=(jax.ShapeDtypeStruct((32, 27), F32), ja...  2.22 us

profile of v2, /device:TPU:1, one launch (start us, length us, event | category | flops | bytes accessed | tf_op | source)
XLA Modules:
  0.0 57.9 jit_solution(2327069498119637703)
XLA Ops:
  0.6 55.1 %shard_map.119 = (f32[2,4,16,16,128]{4,3,2,1,0:T(8,128)}, f32[32,128]{1,0:T(8,128)}) custom-call(bf16[4,32,16,128]{3,2,1,0:T(8,128)(2,1)} %x_hbm.1, bf16[27,32,64]{2,1,0:T(8,128)(2,1)} %bitcast.1, f32[32,32]{1,0:T(8,128)} %gamma_ref.1, f32[32]{0:T(128)} %beta_ref.1, bf16[128,640]{1,0:T(8,128)(2,1)} %hw_hbm.1, f32[640]{0:T(1024)} %hb_ref.1, ...), custom_call_target="tpu_custom_call" | custom-call | tf_op jit(solution)/shard_map/pallas_call | solution.py:760
  55.7 2.2 %shard_map.120 = (f32[32,27]{1,0:T(8,128)}, f32[128,640]{1,0:T(8,128)}, f32[640]{0:T(1024)}, f32[640,256]{1,0:T(8,128)}, f32[256]{0:T(256)}) custom-call(f32[2,4,16,16,128]{4,3,2,1,0:T(8,128)} %get-tuple-element.7.total_ref, f32[32,128]{1,0:T(8,128)} %get-tuple-element.8.block_ref), custom_call_target="tpu_custom_call" | custom-call | tf_op jit(solution)/shard_map/pallas_call | solution.py:773

commit v3 on v2

--- a/solution.py
+++ b/solution.py
@@ -9,6 +9,7 @@
 F32 = jnp.float32
 MESH = pl.DeviceIdType.MESH
 PATCHES = 131072.0
+OFFSETS = [(a, b) for a in range(4) for b in range(4) if a or b]
 
 NN = (((1,), (0,)), ((), ()))
 NT = (((1,), (1,)), ((), ()))
@@ -24,6 +25,11 @@
 
 def onehot(condition):
     return jnp.where(condition, 1.0, 0.0).astype(BF)
+
+
+def tile_spot(t):
+    core, rest = divmod(t, 40)
+    return core, rest // 3, 8 * (rest % 3)
 
 
 def split(value):
@@ -41,8 +47,6 @@
         self.zlo = self.lon // 8
         self.x = self.lat
         self.z = self.ch * 2 + self.zlo
-        self.c1 = jnp.where(self.core == 0, self.x, self.y)
-        self.c2 = jnp.where(self.core == 0, self.y, self.x)
 
     def chip(self, x, y, z, core):
         return ((z % 2) * 8 + y * 2 + core, x, z // 2)
@@ -50,25 +54,36 @@
     def sibling(self):
         return self.chip(self.x, self.y, self.z, 1 - self.core)
 
-    def along_x(self, d):
-        return self.chip((self.x + d) % 4, self.y, self.z, self.core)
-
-    def along_y(self, d):
-        return self.chip(self.x, (self.y + d) % 4, self.z, self.core)
-
     def along_z(self, d):
         return self.chip(self.x, self.y, (self.z + d) % 4, self.core)
 
-    def along_first(self, d):
-        on_x = 1 - self.core
-        return self.chip(
-            (self.x + d * on_x) % 4, (self.y + d * (1 - on_x)) % 4, self.z, self.core
-        )
-
-    def in_plane(self, c2, z):
-        x = jnp.where(self.core == 0, self.x, c2)
-        y = jnp.where(self.core == 0, c2, self.y)
+    def flat(self, a, b):
+        return self.chip((self.x + a) % 4, (self.y + b) % 4, self.z, self.core)
+
+    def plane(self, n, a, b):
+        if n == 1:
+            return self.chip((self.x + a) % 4, self.y, (self.z + b) % 4, self.core)
+        on, off = 1 - self.core, self.core
+        x = (self.x + a * on) % 4
+        y = (self.y + b * on + a * off) % 4
+        z = (self.z + b * off) % 4
         return self.chip(x, y, z, self.core)
+
+    def spot(self, n, a=0, b=0):
+        if n == 1:
+            return ((self.x + a) % 4) * 4 + (self.z + b) % 4
+        first = jnp.where(self.core == 0, self.x, self.y)
+        second = jnp.where(self.core == 0, self.y, self.z)
+        return ((first + a) % 4) * 4 + (second + b) % 4
+
+    def axis(self, n):
+        return self.y if n == 1 else jnp.where(self.core == 0, self.z, self.x)
+
+    def along(self, n, d):
+        if n == 1:
+            return self.flat(0, d)
+        on, off = 1 - self.core, self.core
+        return self.chip((self.x + d * off) % 4, self.y, (self.z + d * on) % 4, self.core)
 
 
 def remote(src, dst, send, recv, device):
@@ -92,31 +107,44 @@
             devices.append(((lon + side) % 16, lat, other))
             devices.append(((lon + side) % 16, row, other))
     devices.append(place.sibling())
-    for d in (1, 2, 3):
-        devices += [place.along_x(d), place.along_y(d), place.along_z(d)]
-    for a in range(1, 4):
-        for d in range(1, 4):
-            devices.append(place.in_plane((place.c2 + a) % 4, (place.z + d) % 4))
+    devices += [place.along_z(d) for d in (1, 2, 3)]
+    devices += [place.flat(a, b) for a, b in OFFSETS]
+    devices += [place.plane(1, a, b) for a, b in OFFSETS if a and b]
     for device in devices:
         pl.semaphore_signal(barrier, inc=1, device_id=device, device_id_type=MESH)
-    return barrier, len(devices)
+
+    @pl.when(place.core == 1)
+    def _():
+        for a, b in OFFSETS:
+            if a and b:
+                pl.semaphore_signal(
+                    barrier, inc=1, device_id=place.plane(0, a, b), device_id_type=MESH
+                )
+
+    return barrier, len(devices) + 9 * place.core
 
 
 def shuffle_latents(x_ref, own, rim_out):
     rows, cols = iota((512, 512), 0), iota((512, 512), 1)
-    swap = onehot(cols == (rows % 32) * 16 + rows // 32)
+    swap = onehot(cols == ((rows & 31) << 4) + (rows >> 5))
     b, n = iota((128, 256), 0), iota((128, 256), 1)
-    parity = jnp.where(n < 64, 2 * n, 2 * (n - 64) + 1)
+    parity = jnp.where(n < 64, 2 * n, 2 * n - 127)
     edge = jnp.where(n < 192, 0, 127)
     spread = onehot(b == jnp.where(n < 128, parity, edge))
     r, j = iota((512, 128), 0), iota((512, 128), 1)
+    slot = (j & 63) - ((r & 15) << 2)
     rims = jnp.zeros((512, 128), F32)
-    for level in range(4):
-        block = mm(x_ref[level].reshape(512, 128), spread)
-        rims = jnp.where((j % 64) == (r % 16) * 4 + level, block[:, 128:], rims)
-        own[level] = mm(swap, block[:, :128].astype(BF)).astype(BF).reshape(16, 32, 128)
+    for pair in range(2):
+        blocks = []
+        for level in (2 * pair, 2 * pair + 1):
+            block = mm(x_ref[level].reshape(512, 128), spread)
+            rims = jnp.where(slot == level, block[:, 128:], rims)
+            blocks.append(block[:, :128].astype(BF))
+        moved = mm(swap, jnp.concatenate(blocks, axis=1)).astype(BF)
+        own[2 * pair] = moved[:, :128].reshape(16, 32, 128)
+        own[2 * pair + 1] = moved[:, 128:].reshape(16, 32, 128)
     c, k = iota((32, 512), 0), iota((32, 512), 1)
-    rim_out[...] = mm(onehot(k // 16 == c), rims.astype(BF)).astype(BF)
+    rim_out[...] = mm(onehot((k >> 4) == c), rims.astype(BF)).astype(BF)
 
 
 def pack_weights(cw_ref, gamma_ref, beta_ref, wl, gb):
@@ -149,14 +177,14 @@
 
 def build_gamma(gall, gam, gamt, beta):
     k, n = iota((128, 256), 0), iota((128, 256), 1)
-    copies = onehot(k == n % 32)
+    copies = onehot(k == (n & 31))
     for g in range(2):
         high, low = split(gall[g])
         for which, part in ((0, high), (1, low)):
             wide = mm(part, copies)
             for s in range(4):
                 block = g * 4 + s
-                own_block = iota((32, 256), 1) // 32 == block
+                own_block = (iota((32, 256), 1) >> 5) == block
                 gam[which, block * 32 : block * 32 + 32, :] = jnp.where(own_block, wide, 0.0)
         for s in range(4):
             block = g * 4 + s
@@ -193,9 +221,9 @@
 def place_rims(place, rim_in, rims):
     chi, lat = place.ch, place.lat
     k, n = iota((512, 128), 0), iota((512, 128), 1)
-    block, kk, nn = k // 128, k % 128, n % 64
+    block, kk, nn = k >> 7, k & 127, n & 63
     left = block < 2
-    same = block % 2 == 0
+    same = (block & 1) == 0
     pole = jnp.where(chi == 0, lat, 3 - lat) == 0
     shift_same = (8 * chi - 1) * 4
     other_low = 36 * chi
@@ -216,7 +244,7 @@
 
 def window_pick():
     col = iota((1, 512), 1)
-    w, js, m = col // 128, (col % 128) // 64, col % 64
+    w, js, m = col >> 7, (col & 127) >> 6, col & 63
     target = jnp.where(
         w == 0,
         jnp.where(m == 0, 256 + js * 8, js * 128 + 63 + m),
@@ -279,7 +307,7 @@
             part = slice(128 * k, 128 * k + 128)
             bias = s["hbt"][part, :]
             pre = mm(s["hwt"][part, :], features) + jnp.concatenate([bias, bias], axis=1)
-            sig = 1.0 / (1.0 + jnp.exp(-pre))
+            sig = 0.5 * jnp.tanh(0.5 * pre) + 0.5
             act = pre * sig
             s["hidden"][part, lanes] = act.astype(BF)
             s["gate"][part, lanes] = sig * (1.0 + pre - act)
@@ -294,8 +322,9 @@
         centre = mm(s["pwt"][0:128, :], hidden) + jnp.concatenate([cb, cb], axis=1)
         raw = mm(s["pwt"][128:256, :], hidden) + jnp.concatenate([rb, rb], axis=1)
         small = jnp.exp(-jnp.abs(raw))
-        spread = 0.5 + jnp.maximum(raw, 0.0) + jnp.log1p(small)
-        sig = jnp.where(raw >= 0.0, 1.0, small) / (1.0 + small)
+        spread = 0.5 + jnp.maximum(raw, 0.0) + jnp.log(1.0 + small)
+        fraction = 1.0 / (1.0 + small)
+        sig = jnp.where(raw >= 0.0, fraction, small * fraction)
         over = 1.0 / spread
         error = (s["normed"][128:256, lanes].astype(F32) - centre) * over
         ratio = error * over * (1.0 / PATCHES)
@@ -310,10 +339,7 @@
 
     grad = mm(s["hidden"][...], s["dparams"][...], NT)
     for half in range(2):
-        for k in range(4):
-            s["part"][half, k, 0:10] = grad[
-                160 * k : 160 * k + 160, 128 * half : 128 * half + 128
-            ].reshape(10, 16, 128)
+        s["ppart"][half] = grad[:, 128 * half : 128 * half + 128].reshape(16, 40, 128)
 
 
 def entropy_backward(s, pw):
@@ -327,20 +353,23 @@
 
 
 def hidden_grads(s):
-    part = s["part"]
+    hpart = s["hpart"]
     ones = jnp.ones((8, 1024), BF)
     pb = mm(ones, s["dparams"][...], NT)
     grad = mm(s["normed"][0:128, :], s["dpre"][...], NT)
-    for k in range(5):
-        for n in range(8):
-            part[n // 4, n % 4, 10 + k] = grad[16 * n : 16 * n + 16, 128 * k : 128 * k + 128]
     hb = mm(ones, s["dpre"][...], NT)
     zeros = jnp.zeros((1, 128), F32)
     lines = [hb[0:1, 128 * k : 128 * k + 128] for k in range(5)]
-    lines += [pb[0:1, 0:128], pb[0:1, 128:256]] + [zeros] * 9
-    for n in range(8):
-        part[n // 4, n % 4, 15] = jnp.zeros((16, 128), F32)
-    part[0, 0, 15] = jnp.concatenate(lines, axis=0)
+    lines += [pb[0:1, 0:128], pb[0:1, 128:256], zeros]
+    for t in range(80):
+        core, place, row = tile_spot(t)
+        n, k = t // 5, t % 5
+        hpart[core, place, row : row + 8] = grad[8 * n : 8 * n + 8, 128 * k : 128 * k + 128]
+    hpart[0, 13, 8:16] = jnp.concatenate(lines, axis=0)
+    hpart[1, 13, 8:16] = jnp.zeros((8, 128), F32)
+    for core in range(2):
+        hpart[core, 13, 16:24] = jnp.zeros((8, 128), F32)
+        hpart[core, 14:16] = jnp.zeros((2, 24, 128), F32)
 
 
 def conv_backward(s, hw):
@@ -375,30 +404,37 @@
                     total = term if total is None else total + term
                 s["wgrad"][32 * g : 32 * g + 32, 192 * n : 192 * n + 192] = total[:, 0:192]
     s["wgrad"][:, 1728:2048] = jnp.zeros((64, 320), F32)
-    for k in range(16):
-        start = 108 * k
-        base = start // 128 * 128
-        shift = (256 - (start - base)) % 256
-        v = s["wgrad"][:, base : base + 256]
-        v = pltpu.roll(v, shift, 1)[:, 0:128] if shift else v[:, 0:128]
-        core, y, zlo = k % 2, (k // 2) % 4, k // 8
+    lane = iota((8, 128), 1) >> 5
+    for k in range(64):
+        first = 27 * k
+        base = first // 128 * 128
+        offset = first - base
+        wide = 128 if offset <= 101 else 256
+        lon, x = k // 4, k % 4
+        core, y, zlo = lon % 2, (lon // 2) % 4, lon // 8
         for g in range(2):
-            s["cpart"][core, g * 2 + zlo, y] = v[32 * g : 32 * g + 32, :]
+            tile = None
+            for q in range(4):
+                v = s["wgrad"][32 * g + 8 * q : 32 * g + 8 * q + 8, base : base + wide]
+                shift = (32 * q - offset) % wide
+                v = pltpu.roll(v, shift, 1)[:, 0:128] if shift else v[:, 0:128]
+                tile = v if tile is None else jnp.where(lane == q, v, tile)
+            s["cpart"][core, g * 2 + zlo, y, x] = tile
 
 
 def body(
     x_hbm, cw_hbm, gamma_ref, beta_ref, hw_hbm, hb_ref, pw_hbm, pb_ref,
-    total_ref, cg_ref,
+    ptotal, htotal, cg_ref,
     x, cw, hw, pw, wl, gb,
     own, rim_out, rim_in, field, wall, gall, rims, pick,
     xt, wf, gam, gamt, beta, hwt, pwt, hbt, pbt,
     conv, inv, normed, hidden, gate, dparams, dtargets, dpre, dconv, taps, wgrad,
-    part, cpart, r1, r2, r3, q1, q2, q3, q4,
-    local_sem, xs, xr, as_, ar, bs, br, gs, gr, cs, cr,
+    ppart, hpart, cpart, pr1, hr1, pr2, hr2, pr3, hr3, q1, q2, q3,
+    local_sem, xs, xr, ks, kr, bs, br, es, er, gs, gr, cs, cr,
 ):
     place = Place()
     lon, lat, chi = place.lon, place.lat, place.ch
-    core, c1, c2, z, y = place.core, place.c1, place.c2, place.z, place.y
+    core, z, y = place.core, place.z, place.y
     partner = (lon, lat, 1 - chi)
     sibling = place.sibling()
     other = 1 - chi
@@ -448,13 +484,15 @@
         remote(own.at[:, 0], field.at[:, chi, 9], xs.at[7], xr.at[7 + chi], (lon, down, 1)),
         remote(own.at[:, 15], field.at[:, chi, 0], xs.at[8], xr.at[7 + chi], (lon, up, 0)),
     )
-    for level in range(4):
-        start(
-            remote(
-                own.at[level, pl.ds(7 * other, 9)], field.at[level, chi, pl.ds(chi, 9)],
-                xs.at[level], xr.at[level], partner,
-            )
+    levels = [
+        remote(
+            own.at[level, pl.ds(7 * other, 9)], field.at[level, chi, pl.ds(chi, 9)],
+            xs.at[level], xr.at[level], partner,
         )
+        for level in range(4)
+    ]
+    levels[0].start()
+    levels[1].start()
     for level in range(4):
         field[level, chi, pl.ds(other, 9)] = own[level, pl.ds(7 * chi, 9)]
     wall[chi] = wl[...]
@@ -466,7 +504,11 @@
     remote(gb, gall.at[other], xs.at[5], xr.at[5], partner).wait_recv()
     remote(wl.at[mine], wall.at[other, mine], xs.at[4], xr.at[4], partner).wait_recv()
     start(remote(wall.at[other, mine], wall.at[other, mine], xs.at[6], xr.at[6], sibling))
+    levels[0].wait_send()
+    levels[2].start()
     build_gamma(gall, gam, gamt, beta)
+    levels[1].wait_send()
+    levels[3].start()
     for half in range(2):
         remote(
             own.at[:, 0], field.at[:, half, 9 * chi], xs.at[7], xr.at[7 + half], partner
@@ -492,7 +534,7 @@
         "xt": xt, "wf": wf, "gam": gam, "gamt": gamt, "beta": beta, "hwt": hwt, "pwt": pwt,
         "hbt": hbt, "pbt": pbt, "conv": conv, "inv": inv, "normed": normed, "hidden": hidden,
         "gate": gate, "dparams": dparams, "dtargets": dtargets, "dpre": dpre, "dconv": dconv,
-        "taps": taps, "wgrad": wgrad, "part": part, "cpart": cpart,
+        "taps": taps, "wgrad": wgrad, "ppart": ppart, "hpart": hpart, "cpart": cpart,
     }
     for level in range(4):
         remote(
@@ -502,129 +544,102 @@
         build_windows(field, rims, pick, xt, level)
         if level >= 1:
             forward(s, level - 1)
+    sends.extend(levels[2:])
     forward(s, 3)
     entropy_forward(s)
 
-    spans = (pl.ds(0, 10), pl.ds(10, 6))
-    p = c2 * 4 + z
+    parts, totals = (ppart, hpart), (ptotal, htotal)
+    firsts, seconds, thirds = (pr1, hr1), (pr2, hr2), (pr3, hr3)
 
     def core_stage(n):
         return start(
-            remote(part.at[1 - core, :, spans[n]], r1.at[:, spans[n]], as_.at[n], ar.at[n], sibling)
+            remote(parts[n].at[1 - core], firsts[n], ks.at[n], kr.at[n], sibling)
         )
 
     def core_add(n):
-        part[core, :, spans[n]] = part[core, :, spans[n]] + r1[:, spans[n]]
-
-    def axis_stage(n):
+        parts[n][core] = parts[n][core] + firsts[n][...]
+
+    def plane_stage(n):
         return start(
             *[
                 remote(
-                    part.at[core, (c1 + d) % 4, spans[n]], r2.at[d - 1, spans[n]],
-                    as_.at[1 + 3 * n + d], ar.at[1 + 3 * n + d], place.along_first(d),
+                    parts[n].at[core, place.spot(n, a, b)], seconds[n].at[4 * a + b],
+                    bs.at[n, 4 * a + b], br.at[n, 4 * a + b], place.plane(n, a, b),
+                )
+                for a, b in OFFSETS
+            ]
+        )
+
+    def plane_add(n):
+        terms = [parts[n][core, place.spot(n)]] + [seconds[n][k] for k in range(1, 16)]
+        while len(terms) > 1:
+            terms = [terms[k] + terms[k + 1] for k in range(0, len(terms), 2)]
+        thirds[n][place.axis(n)] = terms[0]
+
+    def axis_stage(n):
+        axis = place.axis(n)
+        copies = start(
+            *[
+                remote(
+                    thirds[n].at[axis], thirds[n].at[axis],
+                    es.at[n, d], er.at[n, d], place.along(n, d),
                 )
                 for d in (1, 2, 3)
             ]
         )
+        return [
+            remote(
+                thirds[n].at[axis], thirds[n].at[(axis + 4 - d) % 4],
+                es.at[n, d], er.at[n, d], sibling,
+            )
+            for d in (1, 2, 3)
+        ]
 
     def axis_add(n):
-        part[core, c1, spans[n]] = (part[core, c1, spans[n]] + r2[0, spans[n]]) + (
-            r2[1, spans[n]] + r2[2, spans[n]]
-        )
-
-    owners = (range(0, 10), range(10, 16))
-
-    def apart(o, act):
-        pl.when(p != o)(act)
-
-    def plane_copy(o):
-        return remote(
-            part.at[core, c1, o], r3.at[p], bs.at[o], br.at[p], place.in_plane(o // 4, o % 4)
-        )
-
-    def plane_stage(n):
-        for o in owners[n]:
-            apart(o, lambda o=o: plane_copy(o).start())
-
-    def spread_copy(o):
-        view = total_ref.at[core, c1, p]
-        return remote(view, view, gs.at[o], gr.at[p], place.in_plane(o // 4, o % 4))
-
-    def plane_finish(n):
-        @pl.when((p < 10) if n == 0 else (p >= 10))
-        def _():
-            r3[p] = part[core, c1, p]
-            for o in range(16):
-                apart(
-                    o,
-                    lambda o=o: remote(
-                        part.at[core, c1, o], r3.at[o], bs.at[o], br.at[o], sibling
-                    ).wait_recv(),
-                )
-            terms = [r3[o] for o in range(16)]
-            while len(terms) > 1:
-                terms = [terms[k] + terms[k + 1] for k in range(0, len(terms), 2)]
-            total_ref[core, c1, p] = terms[0]
-            for o in range(16):
-                apart(o, lambda o=o: spread_copy(o).start())
-
-    def spread_finish(n):
-        for o in owners[n]:
-            apart(
-                o,
-                lambda o=o: remote(
-                    part.at[core, c1, o], total_ref.at[core, c1, o], gs.at[o], gr.at[o], sibling
-                ).wait_recv(),
-            )
-
-    def axis_spread(n):
-        view = total_ref.at[core, c1, spans[n]]
-        return start(
+        totals[n][core, place.spot(n)] = (thirds[n][0] + thirds[n][1]) + (thirds[n][2] + thirds[n][3])
+
+    def spread_stage(n):
+        view = totals[n].at[core, place.spot(n)]
+        start(
             *[
                 remote(
-                    view, view, as_.at[7 + 3 * n + d], ar.at[7 + 3 * n + d], place.along_first(d)
+                    view, view, gs.at[n, 4 * a + b], gr.at[n, 4 * a + b], place.plane(n, a, b)
                 )
-                for d in (1, 2, 3)
+                for a, b in OFFSETS
             ]
         )
-
-    def axis_arrive(n):
-        for d in (1, 2, 3):
+        return [
             remote(
-                total_ref.at[core, c1, spans[n]],
-                total_ref.at[core, (c1 + 4 - d) % 4, spans[n]],
-                as_.at[7 + 3 * n + d], ar.at[7 + 3 * n + d], sibling,
-            ).wait_recv()
+                view, totals[n].at[core, place.spot(n, 4 - a, 4 - b)],
+                gs.at[n, 4 * a + b], gr.at[n, 4 * a + b], sibling,
+            )
+            for a, b in OFFSETS
+        ]
 
     def core_spread(n):
-        view = total_ref.at[core, :, spans[n]]
-        start(remote(view, view, as_.at[14 + n], ar.at[14 + n], sibling))
-
-    def core_arrive(n):
-        remote(
-            total_ref.at[core, :, spans[n]], total_ref.at[1 - core, :, spans[n]],
-            as_.at[14 + n], ar.at[14 + n], sibling,
-        ).wait_recv()
-
-    going = core_stage(0)
+        view = totals[n].at[core]
+        start(remote(view, view, ks.at[2 + n], kr.at[2 + n], sibling))
+        return [remote(view, totals[n].at[1 - core], ks.at[2 + n], kr.at[2 + n], sibling)]
+
+    core_p = core_stage(0)
     entropy_backward(s, pw)
-    arrive(going)
+    arrive(core_p)
     core_add(0)
-    going_axis = axis_stage(0)
+    plane_p = plane_stage(0)
     hidden_grads(s)
-    going = core_stage(1)
+    core_h = core_stage(1)
     conv_backward(s, hw)
-    arrive(going)
+    arrive(core_h)
     core_add(1)
-    going_axis1 = axis_stage(1)
+    plane_h = plane_stage(1)
     weight_grads(s)
-    going = start(remote(cpart.at[1 - core], q1, cs.at[0], cr.at[0], sibling))
-    arrive(going_axis)
-    axis_add(0)
-    plane_stage(0)
-    arrive(going)
+    core_c = start(remote(cpart.at[1 - core], q1, cs.at[0], cr.at[0], sibling))
+    arrive(plane_p)
+    plane_add(0)
+    axis_p = axis_stage(0)
+    arrive(core_c)
     cpart[core] = cpart[core] + q1[...]
-    going = start(
+    axis_c = start(
         *[
             remote(
                 cpart.at[core, (z + d) % 4], q2.at[d - 1], cs.at[d], cr.at[d], place.along_z(d)
@@ -632,68 +647,56 @@
             for d in (1, 2, 3)
         ]
     )
-    arrive(going_axis1)
+    arrive(plane_h)
+    plane_add(1)
+    axis_h = axis_stage(1)
+    arrive(axis_p)
+    axis_add(0)
+    spread_p = spread_stage(0)
+    arrive(axis_h)
     axis_add(1)
-    plane_stage(1)
-    plane_finish(0)
-    arrive(going)
+    spread_h = spread_stage(1)
+    arrive(axis_c)
     cpart[core, z] = (cpart[core, z] + q2[0]) + (q2[1] + q2[2])
-    going = start(
+    plane_c = start(
         *[
             remote(
-                cpart.at[core, z, (y + d) % 4], q3.at[d - 1], cs.at[3 + d], cr.at[3 + d],
-                place.along_y(d),
+                cpart.at[core, z, (y + b) % 4, (place.x + a) % 4], q3.at[4 * a + b],
+                cs.at[3 + 4 * a + b],
+                cr.at[3 + 4 * a + b], place.flat(a, b),
             )
-            for d in (1, 2, 3)
+            for a, b in OFFSETS
         ]
     )
-    plane_finish(1)
-    spread_finish(0)
-    axis_spread(0)
-    arrive(going)
-    cpart[core, z, y] = (cpart[core, z, y] + q3[0]) + (q3[1] + q3[2])
-    going = start(
-        *[
-            remote(
-                cpart.at[core, z, y], q4.at[d - 1], cs.at[6 + d], cr.at[6 + d], place.along_x(d)
-            )
-            for d in (1, 2, 3)
-        ]
-    )
-    spread_finish(1)
-    axis_spread(1)
-    axis_arrive(0)
-    core_spread(0)
-    arrive(going)
-    block = (cpart[core, z, y] + q4[0]) + (q4[1] + q4[2])
-    cg_ref[...] = pltpu.roll(block, (128 - 27 * place.x) % 128, 1)
-    axis_arrive(1)
-    core_spread(1)
-    core_arrive(0)
-    core_arrive(1)
+    arrive(spread_p)
+    core_p = core_spread(0)
+    arrive(spread_h)
+    core_h = core_spread(1)
+    arrive(plane_c)
+    terms = [cpart[core, z, y, place.x]] + [q3[k] for k in range(1, 16)]
+    while len(terms) > 1:
+        terms = [terms[k] + terms[k + 1] for k in range(0, len(terms), 2)]
+    for q in range(4):
+        v = pltpu.roll(terms[0], 128 - 32 * q, 1) if q else terms[0]
+        cg_ref[8 * q : 8 * q + 8, :] = v
+    arrive(core_p)
+    arrive(core_h)
     for copy in sends:
         copy.wait_send()
-    for o in range(16):
-        apart(o, lambda o=o: plane_copy(o).wait_send())
-        apart(o, lambda o=o: spread_copy(o).wait_send())
-
-
-def unpack(total_ref, block_ref, cg_ref, hwg_ref, hbg_ref, pwg_ref, pbg_ref):
+
+
+def unpack(ptotal, htotal, block_ref, cg_ref, hwg_ref, hbg_ref, pwg_ref, pbg_ref):
     cg_ref[...] = block_ref[:, 0:27]
     for half in range(2):
-        for k in range(4):
-            pwg_ref[160 * k : 160 * k + 160, 128 * half : 128 * half + 128] = total_ref[
-                half, k, 0:10
-            ].reshape(160, 128)
-    for n in range(8):
-        for k in range(5):
-            hwg_ref[16 * n : 16 * n + 16, 128 * k : 128 * k + 128] = total_ref[
-                n // 4, n % 4, 10 + k
-            ]
+        pwg_ref[:, 128 * half : 128 * half + 128] = ptotal[half].reshape(640, 128)
+    for t in range(80):
+        core, place, row = tile_spot(t)
+        n, k = t // 5, t % 5
+        hwg_ref[8 * n : 8 * n + 8, 128 * k : 128 * k + 128] = htotal[core, place, row : row + 8]
     for k in range(5):
-        hbg_ref[128 * k : 128 * k + 128] = total_ref[0, 0, 15, k]
+        hbg_ref[128 * k : 128 * k + 128] = htotal[0, 13, 8 + k]
     for k in range(2):
-        pbg_ref[128 * k : 128 * k + 128] = total_ref[0, 0, 15, 5 + k]
+        pbg_ref[128 * k : 128 * k + 128] = htotal[0, 13, 13 + k]
 
 
 def on_device(x, cw, gamma, beta, hw, hb, pw, pb):
@@ -734,37 +737,43 @@
         vmem((256, 1024), BF),
         vmem((3, 256, 1024), F32),
         vmem((64, 2048), F32),
-        vmem((2, 4, 16, 16, 128), F32),
-        vmem((2, 4, 4, 32, 128), F32),
-        vmem((4, 16, 16, 128), F32),
-        vmem((3, 16, 16, 128), F32),
-        vmem((16, 16, 128), F32),
-        vmem((4, 4, 32, 128), F32),
-        vmem((3, 4, 32, 128), F32),
-        vmem((3, 32, 128), F32),
-        vmem((3, 32, 128), F32),
+        vmem((2, 16, 40, 128), F32),
+        vmem((2, 16, 24, 128), F32),
+        vmem((2, 4, 4, 4, 8, 128), F32),
+        vmem((16, 40, 128), F32),
+        vmem((16, 24, 128), F32),
+        vmem((16, 40, 128), F32),
+        vmem((16, 24, 128), F32),
+        vmem((4, 40, 128), F32),
+        vmem((4, 24, 128), F32),
+        vmem((4, 4, 4, 8, 128), F32),
+        vmem((3, 4, 4, 8, 128), F32),
+        vmem((16, 8, 128), F32),
         dma((4,)),
         dma((17,)),
         dma((17,)),
-        dma((16,)),
-        dma((16,)),
-        dma((16,)),
-        dma((16,)),
-        dma((16,)),
-        dma((16,)),
-        dma((10,)),
-        dma((10,)),
+        dma((4,)),
+        dma((4,)),
+        dma((2, 16)),
+        dma((2, 16)),
+        dma((2, 4)),
+        dma((2, 4)),
+        dma((2, 16)),
+        dma((2, 16)),
+        dma((19,)),
+        dma((19,)),
     ]
     spec = pl.BlockSpec(memory_space=pltpu.VMEM)
     anywhere = pl.BlockSpec(memory_space=pl.ANY)
-    total, block = pl.pallas_call(
+    ptotal, htotal, block = pl.pallas_call(
         body,
         out_shape=(
-            jax.ShapeDtypeStruct((2, 4, 16, 16, 128), F32),
+            jax.ShapeDtypeStruct((2, 16, 40, 128), F32),
+            jax.ShapeDtypeStruct((2, 16, 24, 128), F32),
             jax.ShapeDtypeStruct((32, 128), F32),
         ),
         in_specs=[anywhere, anywhere, spec, spec, anywhere, spec, anywhere, spec],
-        out_specs=(spec, spec),
+        out_specs=(spec, spec, spec),
         scratch_shapes=scratch,
         compiler_params=pltpu.CompilerParams(
             collective_id=0, has_side_effects=True, vmem_limit_bytes=56 * 1024 * 1024
@@ -779,9 +788,9 @@
             jax.ShapeDtypeStruct((640, 256), F32),
             jax.ShapeDtypeStruct((256,), F32),
         ),
-        in_specs=[spec] * 2,
+        in_specs=[spec] * 3,
         out_specs=(spec,) * 5,
-    )(total, block)
+    )(ptotal, htotal, block)
 
 
 def solution(mesh):

time: 58.1 us -> 54.7 us (0.941)
  Pallas kernels: 57.3 us -> 53.9 us
    pallas_call x1, Pallas kernels: 55.1 us -> 51.7 us  [on_device(): pl.pallas_call(body, out_shape=(jax.ShapeDtypeStruct((2, 16, 40, 128), F3...]
where the time goes in v3:
time: 54.7 us; the launch traced here: 54.5 us
  Pallas kernels  53.9 us (99%)
  between operations  0.64 us (1%)
    pallas_call x1, Pallas kernels, on_device(): pl.pallas_call(body, out_shape=(jax.ShapeDtypeStruct((2, 16, 40, 128), F3...  51.7 us
    pallas_call x1, Pallas kernels, on_device(): pl.pallas_call(unpack, out_shape=(jax.ShapeDtypeStruct((32, 27), F32), ja...  2.21 us

profile of v3, /device:TPU:1, one launch (start us, length us, event | category | flops | bytes accessed | tf_op | source)
XLA Modules:
  0.0 54.5 jit_solution(13284405533070261567)
XLA Ops:
  0.6 51.7 %shard_map.119 = (f32[2,16,40,128]{3,2,1,0:T(8,128)}, f32[2,16,24,128]{3,2,1,0:T(8,128)}, f32[32,128]{1,0:T(8,128)}) custom-call(bf16[4,32,16,128]{3,2,1,0:T(8,128)(2,1)} %x_hbm.1, bf16[27,32,64]{2,1,0:T(8,128)(2,1)} %bitcast.1, f32[32,32]{1,0:T(8,128)} %gamma_ref.1, f32[32]{0:T(128)} %beta_ref.1, bf16[128,640]{1,0:T(8,128)(2,1)} %hw_hbm.1, f32[640]{0:T(1024)} %hb_ref.1, ...), custom_call_target="tpu_custom_call" | custom-call | tf_op jit(solution)/shard_map/pallas_call | solution.py:768
  52.3 2.2 %shard_map.120 = (f32[32,27]{1,0:T(8,128)}, f32[128,640]{1,0:T(8,128)}, f32[640]{0:T(1024)}, f32[640,256]{1,0:T(8,128)}, f32[256]{0:T(256)}) custom-call(f32[2,16,40,128]{3,2,1,0:T(8,128)} %get-tuple-element.8.ptotal, f32[2,16,24,128]{3,2,1,0:T(8,128)} %get-tuple-element.9.htotal, f32[32,128]{1,0:T(8,128)} %get-tuple-element.10.block_ref), custom_call_target="tpu_custom_call" | custom-call | tf_op jit(solution)/shard_map/pallas_call | solution.py:782

commit v4 on v3

--- a/solution.py
+++ b/solution.py
@@ -634,9 +634,6 @@
     plane_h = plane_stage(1)
     weight_grads(s)
     core_c = start(remote(cpart.at[1 - core], q1, cs.at[0], cr.at[0], sibling))
-    arrive(plane_p)
-    plane_add(0)
-    axis_p = axis_stage(0)
     arrive(core_c)
     cpart[core] = cpart[core] + q1[...]
     axis_c = start(
@@ -647,15 +644,12 @@
             for d in (1, 2, 3)
         ]
     )
+    arrive(plane_p)
+    plane_add(0)
+    axis_p = axis_stage(0)
     arrive(plane_h)
     plane_add(1)
     axis_h = axis_stage(1)
-    arrive(axis_p)
-    axis_add(0)
-    spread_p = spread_stage(0)
-    arrive(axis_h)
-    axis_add(1)
-    spread_h = spread_stage(1)
     arrive(axis_c)
     cpart[core, z] = (cpart[core, z] + q2[0]) + (q2[1] + q2[2])
     plane_c = start(
@@ -668,10 +662,12 @@
             for a, b in OFFSETS
         ]
     )
-    arrive(spread_p)
-    core_p = core_spread(0)
-    arrive(spread_h)
-    core_h = core_spread(1)
+    arrive(axis_p)
+    axis_add(0)
+    spread_p = spread_stage(0)
+    arrive(axis_h)
+    axis_add(1)
+    spread_h = spread_stage(1)
     arrive(plane_c)
     terms = [cpart[core, z, y, place.x]] + [q3[k] for k in range(1, 16)]
     while len(terms) > 1:
@@ -679,6 +675,10 @@
     for q in range(4):
         v = pltpu.roll(terms[0], 128 - 32 * q, 1) if q else terms[0]
         cg_ref[8 * q : 8 * q + 8, :] = v
+    arrive(spread_p)
+    core_p = core_spread(0)
+    arrive(spread_h)
+    core_h = core_spread(1)
     arrive(core_p)
     arrive(core_h)
     for copy in sends:

time: 54.7 us -> 56.5 us (1.033)
  Pallas kernels: 53.9 us -> 55.6 us
    pallas_call x1, Pallas kernels: 51.7 us -> 53.4 us  [on_device(): pl.pallas_call(body, out_shape=(jax.ShapeDtypeStruct((2, 16, 40, 128), F3...]
where the time goes in v4:
time: 56.5 us; the launch traced here: 56.3 us
  Pallas kernels  55.6 us (98%)
  between operations  0.64 us (1%)
    pallas_call x1, Pallas kernels, on_device(): pl.pallas_call(body, out_shape=(jax.ShapeDtypeStruct((2, 16, 40, 128), F3...  53.4 us
    pallas_call x1, Pallas kernels, on_device(): pl.pallas_call(unpack, out_shape=(jax.ShapeDtypeStruct((32, 27), F32), ja...  2.21 us

profile of v4, /device:TPU:1, one launch (start us, length us, event | category | flops | bytes accessed | tf_op | source)
XLA Modules:
  0.0 56.3 jit_solution(664351312332663701)
XLA Ops:
  0.6 53.4 %shard_map.119 = (f32[2,16,40,128]{3,2,1,0:T(8,128)}, f32[2,16,24,128]{3,2,1,0:T(8,128)}, f32[32,128]{1,0:T(8,128)}) custom-call(bf16[4,32,16,128]{3,2,1,0:T(8,128)(2,1)} %x_hbm.1, bf16[27,32,64]{2,1,0:T(8,128)(2,1)} %bitcast.1, f32[32,32]{1,0:T(8,128)} %gamma_ref.1, f32[32]{0:T(128)} %beta_ref.1, bf16[128,640]{1,0:T(8,128)(2,1)} %hw_hbm.1, f32[640]{0:T(1024)} %hb_ref.1, ...), custom_call_target="tpu_custom_call" | custom-call | tf_op jit(solution)/shard_map/pallas_call | solution.py:768
  54.1 2.2 %shard_map.120 = (f32[32,27]{1,0:T(8,128)}, f32[128,640]{1,0:T(8,128)}, f32[640]{0:T(1024)}, f32[640,256]{1,0:T(8,128)}, f32[256]{0:T(256)}) custom-call(f32[2,16,40,128]{3,2,1,0:T(8,128)} %get-tuple-element.8.ptotal, f32[2,16,24,128]{3,2,1,0:T(8,128)} %get-tuple-element.9.htotal, f32[32,128]{1,0:T(8,128)} %get-tuple-element.10.block_ref), custom_call_target="tpu_custom_call" | custom-call | tf_op jit(solution)/shard_map/pallas_call | solution.py:782

commit v5 on v3

--- a/solution.py
+++ b/solution.py
@@ -179,20 +179,19 @@
     k, n = iota((128, 256), 0), iota((128, 256), 1)
     copies = onehot(k == (n & 31))
     for g in range(2):
-        high, low = split(gall[g])
-        for which, part in ((0, high), (1, low)):
+        for which, part in enumerate(split(gall[g])):
             wide = mm(part, copies)
-            for s in range(4):
-                block = g * 4 + s
+            for block in range(4 * g, 4 * g + 4):
                 own_block = (iota((32, 256), 1) >> 5) == block
-                gam[which, block * 32 : block * 32 + 32, :] = jnp.where(own_block, wide, 0.0)
-        for s in range(4):
-            block = g * 4 + s
+                row = 256 * which + 32 * block
+                gam[row : row + 32, :] = jnp.where(own_block, wide, 0.0).astype(BF)
+        for block in range(4 * g, 4 * g + 4):
             beta[block * 32 : block * 32 + 32, :] = jnp.broadcast_to(
                 gall[g][:, 64:65], (32, 256)
             )
     for which in range(2):
-        gamt[which] = gam[which].T
+        part = slice(256 * which, 256 * which + 256)
+        gamt[part, :] = gam[part, :].astype(F32).T.astype(BF)
 
 
 def build_weights(wall, wf):
@@ -281,8 +280,8 @@
 
 def mix(gam, value):
     high, low = split(value)
-    ghigh, glow = gam[0].astype(BF), gam[1].astype(BF)
-    return mm(ghigh, high) + (mm(ghigh, low) + mm(glow, high))
+    both = mm(gam[...], high)
+    return both[0:256, :] + (both[256:512, :] + mm(gam[0:256, :], low))
 
 
 def forward(s, level):
@@ -719,8 +718,8 @@
         vmem((384, 512), BF),
         vmem((1024, 1024), BF),
         vmem((3, 256, 1024), BF),
-        vmem((2, 256, 256), F32),
-        vmem((2, 256, 256), F32),
+        vmem((512, 256), BF),
+        vmem((512, 256), BF),
         vmem((256, 256), F32),
         vmem((640, 128), BF),
         vmem((256, 640), BF),

time: 54.7 us -> 54.8 us (level)
  no operation moved by 1% of the time
where the time goes in v5:
time: 54.8 us; the launch traced here: 54.5 us
  Pallas kernels  53.9 us (98%)
  between operations  0.64 us (1%)
    pallas_call x1, Pallas kernels, on_device(): pl.pallas_call(body, out_shape=(jax.ShapeDtypeStruct((2, 16, 40, 128), F3...  51.7 us
    pallas_call x1, Pallas kernels, on_device(): pl.pallas_call(unpack, out_shape=(jax.ShapeDtypeStruct((32, 27), F32), ja...  2.21 us

profile of v5, /device:TPU:1, one launch (start us, length us, event | category | flops | bytes accessed | tf_op | source)
XLA Modules:
  0.0 54.5 jit_solution(260940077787204568)
XLA Ops:
  0.6 51.7 %shard_map.119 = (f32[2,16,40,128]{3,2,1,0:T(8,128)}, f32[2,16,24,128]{3,2,1,0:T(8,128)}, f32[32,128]{1,0:T(8,128)}) custom-call(bf16[4,32,16,128]{3,2,1,0:T(8,128)(2,1)} %x_hbm.1, bf16[27,32,64]{2,1,0:T(8,128)(2,1)} %bitcast.1, f32[32,32]{1,0:T(8,128)} %gamma_ref.1, f32[32]{0:T(128)} %beta_ref.1, bf16[128,640]{1,0:T(8,128)(2,1)} %hw_hbm.1, f32[640]{0:T(1024)} %hb_ref.1, ...), custom_call_target="tpu_custom_call" | custom-call | tf_op jit(solution)/shard_map/pallas_call | solution.py:767
  52.3 2.2 %shard_map.120 = (f32[32,27]{1,0:T(8,128)}, f32[128,640]{1,0:T(8,128)}, f32[640]{0:T(1024)}, f32[640,256]{1,0:T(8,128)}, f32[256]{0:T(256)}) custom-call(f32[2,16,40,128]{3,2,1,0:T(8,128)} %get-tuple-element.8.ptotal, f32[2,16,24,128]{3,2,1,0:T(8,128)} %get-tuple-element.9.htotal, f32[32,128]{1,0:T(8,128)} %get-tuple-element.10.block_ref), custom_call_target="tpu_custom_call" | custom-call | tf_op jit(solution)/shard_map/pallas_call | solution.py:781
